TPU v7x, 512 devices: a whole 4x8x8 slice. The times are simulated.
512 devices in a mesh: gx: 8 (over x, core), gy: 4 (over z_hi), gz: 16 (over z_lo, y).
Axes of the slice: x: 4, y: 8, z: 8 (z_hi: 4, z_lo: 2; z = z_hi * 2 + z_lo), core: 2. Of those that a mesh axis runs over, the one named last changes fastest.
Arguments:
- density: float32 [16, 32, 96, 1024], P('gz', 'gy', None, 'gx'), may hold values from 0.2 to 1
- bone: int32 [16, 32, 96, 1024], P('gz', 'gy', None, 'gx'), may hold values 0 or 1
- fixed: int32 [16, 32, 96, 1024], P('gz', 'gy', None, 'gx'), may hold values 0 or 1
- load: float32 [3, 16, 32, 96, 1024], P(None, 'gz', 'gy', None, 'gx'), may hold values from -6 to 6
Outputs:
- density_new: float32 [16, 32, 96, 1024], P('gz', 'gy', None, 'gx')
- displacement: float32 [3, 16, 32, 96, 1024], P(None, 'gz', 'gy', None, 'gx')
All inputs are finite; a program needn't handle non-finite values. No bound on the sum of `bone` or of `fixed` on one device may be relied on, other than what follows from the above.
Results may differ from a plain program's by a relative error of at most 0.00024.
Values sent between devices are 32-bit elements; how exact they have to be, the bound alone decides.
A program may use at most 64 MiB of HBM per device.

v0:
```python
import math

import jax
import jax.numpy as jnp
import numpy as np
from jax import lax
from jax.sharding import PartitionSpec as P

RAD = 24
ITERS = 2


MARROW = 0.1
REMODEL = 0.25
FLOOR = 0.2
CEILING = 1.0
EPSILON = 1e-06


def shifted(value, axis, steps):
    count = lax.axis_size(axis)
    initial, last = (max(0, -steps), min(count, count - steps))
    return lax.ppermute(value, axis, [(source, source + steps) for source in range(initial, last)])


def from_behind(block, axis, distance):
    devices = range(lax.axis_size(axis))
    route = [((i - distance) % len(devices), i) for i in devices]
    return lax.ppermute(block, axis, route)


def extended(block, sides, width):
    for axis, dim in sides:
        count = lax.axis_size(axis)
        forward = [(i, i + 1) for i in range(count - 1)]
        backward = [(target, source) for source, target in forward]
        low = lax.ppermute(
            lax.slice_in_dim(block, block.shape[dim] - width, None, axis=dim), axis, forward
        )
        high = lax.ppermute(lax.slice_in_dim(block, 0, width, axis=dim), axis, backward)
        block = jnp.concatenate([low, block, high], axis=dim)
    return block


def element_stiffness():
    poisson = 0.3
    lame = poisson / ((1.0 + poisson) * (1.0 - 2.0 * poisson))
    shear = 0.5 / (1.0 + poisson)
    elastic = np.zeros((6, 6))
    elastic[:3, :3] = lame
    for index in range(3):
        elastic[index, index] += 2.0 * shear
        elastic[index + 3, index + 3] = shear
    points = [0.5 - 0.5 / math.sqrt(3.0), 0.5 + 0.5 / math.sqrt(3.0)]
    matrix = np.zeros((24, 24))
    for point_z in points:
        for point_y in points:
            for point_x in points:
                strain = np.zeros((6, 24))
                for corner_z in range(2):
                    for corner_y in range(2):
                        for corner_x in range(2):
                            node = 4 * corner_z + 2 * corner_y + corner_x
                            shape_x = point_x if corner_x else 1.0 - point_x
                            shape_y = point_y if corner_y else 1.0 - point_y
                            shape_z = point_z if corner_z else 1.0 - point_z
                            slope_x = 1.0 if corner_x else -1.0
                            slope_y = 1.0 if corner_y else -1.0
                            slope_z = 1.0 if corner_z else -1.0
                            along_x = slope_x * shape_y * shape_z
                            along_y = shape_x * slope_y * shape_z
                            along_z = shape_x * shape_y * slope_z
                            strain[0, node] = along_x
                            strain[1, 8 + node] = along_y
                            strain[2, 16 + node] = along_z
                            strain[3, node] = along_y
                            strain[3, 8 + node] = along_x
                            strain[4, 8 + node] = along_z
                            strain[4, 16 + node] = along_y
                            strain[5, node] = along_z
                            strain[5, 16 + node] = along_x
                matrix = matrix + strain.T @ elastic @ strain / 8.0
    return matrix


def corners():
    return [
        (corner_z, corner_y, corner_x)
        for corner_z in range(2)
        for corner_y in range(2)
        for corner_x in range(2)
    ]


def corner_values(nodes, depth, height, width):
    values = []
    for component in range(3):
        for cz, cy, cx in corners():
            values.append(nodes[component, cz : cz + depth, cy : cy + height, cx : cx + width])
    return values


def element_rows(values, table):
    products = []
    for row in range(24):
        total = values[0] * float(table[row, 0])
        for column in range(1, 24):
            total = total + values[column] * float(table[row, column])
        products.append(total)
    return products


def lean_forces(nodes, moduli, table):
    depth, height, width = moduli.shape
    products = element_rows(corner_values(nodes, depth, height, width), table)
    components = []
    for component in range(3):
        total = jnp.zeros((depth + 1, height + 1, width + 1), jnp.float32)
        for node, (cz, cy, cx) in enumerate(corners()):
            term = moduli * products[component * 8 + node]
            total = total + jnp.pad(term, ((cz, 1 - cz), (cy, 1 - cy), (cx, 1 - cx)))
        components.append(total)
    return jnp.stack(components, axis=0)


def lean_energy(nodes, moduli, table):
    depth, height, width = moduli.shape
    values = corner_values(nodes, depth, height, width)
    products = element_rows(values, table)
    total = values[0] * products[0]
    for row in range(1, 24):
        total = total + values[row] * products[row]
    return 0.5 * moduli * total


def stiffness_diagonal(moduli_ext, stiffness, depth, height, width):
    main = jnp.diagonal(stiffness).reshape(3, 8)
    total = jnp.zeros((3, depth, height, width), jnp.float32)
    for node, (cz, cy, cx) in enumerate(corners()):
        piece = moduli_ext[
            1 - cz : 1 - cz + depth, 1 - cy : 1 - cy + height, 1 - cx : 1 - cx + width
        ]
        total = total + main[:, node][:, None, None, None] * piece[None]
    return total


def banded(length_in, length_out, radius):
    offsets = jnp.arange(2 * radius + 1).astype(jnp.float32) - radius
    normal = jnp.sum(jnp.exp(-jnp.abs(offsets) / (0.5 * radius)))
    inputs = jnp.arange(length_in)[:, None]
    outputs = jnp.arange(length_out)[None, :]
    distance = (inputs - (length_in - length_out) // 2 - outputs).astype(jnp.float32)
    weight = jnp.exp(-jnp.abs(distance) / (0.5 * radius)) / normal
    return jnp.where(jnp.abs(distance) <= radius, weight, 0.0)


def smooth(values, axis, length_out):
    matrix = banded(values.shape[axis], length_out, RAD)
    if axis == 2:
        return jnp.einsum("zyi,io->zyo", values, matrix, precision=lax.Precision.HIGHEST)
    if axis == 1:
        return jnp.einsum("zix,io->zox", values, matrix, precision=lax.Precision.HIGHEST)
    return jnp.einsum("iyx,io->oyx", values, matrix, precision=lax.Precision.HIGHEST)


def upper_nodes(field):
    column = shifted(field[:, :, :, :1], "gx", -1)
    wide = jnp.concatenate([field, column], axis=3)
    inner = from_behind(wide[:, :1], "gy", -1)
    outer = shifted(inner, "gz", -1)
    position = lax.axis_index("gy")
    upper = jnp.where(position == lax.axis_size("gy") - 1, outer, inner)
    return jnp.concatenate([wide, upper], axis=1)


def fold_upper(values):
    depth = values.shape[1] - 1
    width = values.shape[3] - 1
    inner = from_behind(values[:, depth:], "gy", 1)
    outer = shifted(inner, "gz", 1)
    position = lax.axis_index("gy")
    carried = jnp.where(position == 0, outer, inner)
    values = jnp.concatenate([values[:, :1] + carried, values[:, 1:depth]], axis=1)
    column = shifted(values[:, :, :, width:], "gx", 1)
    return jnp.concatenate([values[:, :, :, :1] + column, values[:, :, :, 1:width]], axis=3)


def node_forces(field, modulus, table):
    height = field.shape[2]
    nodes = jnp.pad(upper_nodes(field), ((0, 0), (0, 0), (0, 1), (0, 0)))
    forces = lean_forces(nodes, modulus, table)
    return fold_upper(forces[:, :, :height])


def local_energy(solution, modulus, table):
    nodes = jnp.pad(upper_nodes(solution), ((0, 0), (0, 0), (0, 1), (0, 0)))
    return lean_energy(nodes, modulus, table)


def inner_sum(values):
    return lax.psum(jnp.sum(values), ("gx", "gy", "gz"))


def to_bricks(values):
    return lax.all_to_all(values, "gy", split_axis=2, concat_axis=1, tiled=True)


def to_slabs(values):
    return lax.all_to_all(values, "gy", split_axis=1, concat_axis=2, tiled=True)


def on_device(density, bone, fixed, load):
    table = element_stiffness()
    stiffness = jnp.asarray(table, jnp.float32)
    local_density = density[0]
    bone_share = bone[0].astype(jnp.float32)
    free_nodes = 1.0 - fixed[0].astype(jnp.float32)
    modulus = bone_share * local_density * local_density + (1.0 - bone_share) * MARROW
    depth, height, width = local_density.shape
    moduli_ext = jnp.pad(modulus, ((1, 1), (1, 0), (1, 1)))
    diagonal_part = stiffness_diagonal(moduli_ext, stiffness, depth + 1, height, width + 1)
    precondition = free_nodes / fold_upper(diagonal_part)
    residual = free_nodes * load[:, 0]
    solution = jnp.zeros_like(residual)
    search = precondition * residual
    gamma = inner_sum(residual * search)
    for count in range(ITERS):
        image = free_nodes * node_forces(free_nodes * search, modulus, table)
        alpha = gamma / lax.psum(jnp.sum(search * image), ("gx", "gy", "gz"))
        solution = solution + alpha * search
        if count + 1 < ITERS:
            residual = residual - alpha * image
            scaled = precondition * residual
            gamma_next = inner_sum(residual * scaled)
            search = scaled + gamma_next / gamma * search
            gamma = gamma_next
    energy = local_energy(solution, modulus, table)
    specific = energy / local_density
    brick = to_bricks(specific[None])[0]
    extent = brick.shape
    beside_all = extended(brick, (("gx", 2), ("gy", 1), ("gz", 0)), RAD)
    stimulus = smooth(smooth(smooth(beside_all, 2, extent[2]), 1, extent[1]), 0, extent[0])
    total = lax.psum(jnp.sum(stimulus), ("gx", "gy", "gz"))
    cells = stimulus.size * lax.axis_size("gx") * lax.axis_size("gy") * lax.axis_size("gz")
    mean = total / cells
    returned = to_slabs(stimulus[None])[0]
    updated = local_density + REMODEL * bone_share * (returned / (mean + EPSILON) - 1.0)
    updated = jnp.clip(updated, FLOOR, CEILING)
    return (updated[None], solution[:, None])


def solution(mesh):
    placed = (
        P("gz", "gy", None, "gx"),
        P("gz", "gy", None, "gx"),
        P("gz", "gy", None, "gx"),
        P(None, "gz", "gy", None, "gx"),
    )
    return jax.shard_map(
        on_device,
        mesh=mesh,
        in_specs=placed,
        out_specs=(P("gz", "gy", None, "gx"), P(None, "gz", "gy", None, "gx")),
        check_vma=False,
    )
```

profile of v0, /device:TPU:1, one launch (start us, length us, event | category | flops | bytes accessed | tf_op | source)
XLA Modules:
  0.0 883.7 jit_solution(2962526408976098601)
XLA Ops:
  1.9 3.2 pad_slice_fusion.9
  6.2 3.6 multiply_add_fusion
  9.8 6.6 collective-permute-start
  16.7 11.0 %collective-permute-done = f32[3,1,96,129]{3,2,1,0:T(8,128)S(1)} collective-permute-done((f32[3,1,96,129]{3,2,1,0:T(8,128)S(1)}, f32[3,1,96,129]{3,2,1,0:T(8,128)S(1)}, u32[]{:S(2)}, u32[]{:S(2)}) %collective-permute-start) | collective-permute-done | bytes 148640 | tf_op jit(solution)/shard_map/ppermute | solution.py:29
  27.7 3.7 collective-permute-start.1
  31.5 5.0 collective-permute-done.1
  40.2 5.2 collective-permute-start.2
  53.6 3.1 collective-permute-done.3
  59.1 10.1 %collective-permute-start.4 = (f32[3,1,96,129]{3,2,1,0:T(8,128)S(1)}, f32[3,1,96,129]{3,2,1,0:T(8,128)S(1)}, u32[]{:S(2)}, u32[]{:S(2)}) collective-permute-start(f32[3,1,96,129]{3,2,1,0:T(8,128)S(1)} %pad_maximum_fusion.19), channel_id=1, source_target_pairs={{16,0},{32,16},{48,32},{0,48},{17,1},{33,17},{49,33},{1,49},{18,2}... | collective-permute-start | bytes 445832 | tf_op jit(solution)/shard_map/ppermute | solution.py:29
  69.2 11.7 %collective-permute-done.4 = f32[3,1,96,129]{3,2,1,0:T(8,128)S(1)} collective-permute-done((f32[3,1,96,129]{3,2,1,0:T(8,128)S(1)}, f32[3,1,96,129]{3,2,1,0:T(8,128)S(1)}, u32[]{:S(2)}, u32[]{:S(2)}) %collective-permute-start.4) | collective-permute-done | bytes 148640 | tf_op jit(solution)/shard_map/ppermute | solution.py:29
  82.6 8.8 %collective-permute-done.5 = f32[3,1,96,129]{3,2,1,0:T(8,128)} collective-permute-done((f32[3,1,96,129]{3,2,1,0:T(8,128)S(1)}, f32[3,1,96,129]{3,2,1,0:T(8,128)}, u32[]{:S(2)}, u32[]{:S(2)}) %collective-permute-start.5) | collective-permute-done | bytes 148640 | tf_op jit(solution)/shard_map/ppermute | solution.py:23
  128.6 3.9 collective-permute-start.6
  132.5 12.3 %collective-permute-done.6 = f32[3,1,96,129]{3,2,1,0:T(8,128)S(1)} collective-permute-done((f32[3,1,96,129]{3,2,1,0:T(8,128)S(1)}, f32[3,1,96,129]{3,2,1,0:T(8,128)S(1)}, u32[]{:S(2)}, u32[]{:S(2)}) %collective-permute-start.6) | collective-permute-done | bytes 148640 | tf_op jit(solution)/shard_map/ppermute | solution.py:29
  144.8 6.2 collective-permute-start.7
  151.0 5.9 collective-permute-done.7
  159.2 5.2 collective-permute-start.8
  164.4 3.1 slice_bitcast_fusion
  172.5 99.2 %all-reduce.52 = (f32[]{:T(128)}, f32[]{:T(128)}) all-reduce(f32[]{:T(128)} %get-tuple-element.11, f32[]{:T(128)} %get-tuple-element.10), channel_id=1, replica_groups=mesh['gx'=8,'gy'=4,'gz'=16] {'gx','gy','gz'}, use_global_device_ids=true, to_apply=%region_2.3 | all-reduce | flops 2 | bytes 16 | tf_op jit(solution)/shard_map/psum | solution.py:201
  273.0 4.8 multiply_reduce_fusion
  277.8 95.7 %psum.37 = f32[]{:T(128)} all-reduce(f32[]{:T(128)} %get-tuple-element.26), channel_id=1, replica_groups=mesh['gx'=8,'gy'=4,'gz'=16] {'gx','gy','gz'}, use_global_device_ids=true, to_apply=%region_6.7 | all-reduce | flops 1 | bytes 8 | tf_op jit(solution)/shard_map/psum | solution.py:201
  384.1 3.1 collective-permute-start.10
  387.2 10.5 %collective-permute-done.10 = f32[3,1,96,129]{3,2,1,0:T(8,128)S(1)} collective-permute-done((f32[3,1,96,129]{3,2,1,0:T(8,128)S(1)}, f32[3,1,96,129]{3,2,1,0:T(8,128)S(1)}, u32[]{:S(2)}, u32[]{:S(2)}) %collective-permute-start.10) | collective-permute-done | bytes 148640 | tf_op jit(solution)/shard_map/ppermute | solution.py:29
  399.2 11.4 %collective-permute-done.11 = f32[3,1,96,129]{3,2,1,0:T(8,128)S(1)} collective-permute-done((f32[3,1,96,129]{3,2,1,0:T(8,128)S(1)}, f32[3,1,96,129]{3,2,1,0:T(8,128)S(1)}, u32[]{:S(2)}, u32[]{:S(2)}) %collective-permute-start.11) | collective-permute-done | bytes 148640 | tf_op jit(solution)/shard_map/ppermute | solution.py:23
  446.7 4.3 collective-permute-start.12
  451.0 7.4 collective-permute-done.12
  458.4 3.6 collective-permute-start.13
  462.0 3.9 collective-permute-done.13
  468.3 6.7 collective-permute-start.14
  480.9 2.7 fusion.20
  483.6 104.0 %psum.38 = f32[]{:T(128)} all-reduce(f32[]{:T(128)} %fusion.20), channel_id=1, replica_groups=mesh['gx'=8,'gy'=4,'gz'=16] {'gx','gy','gz'}, use_global_device_ids=true, to_apply=%region_8.9 | all-reduce | flops 1 | bytes 8 | tf_op jit(solution)/shard_map/psum | solution.py:229
  593.3 3.0 collective-permute-done.15
  596.8 3.0 collective-permute-start.16
  599.9 8.4 collective-permute-done.16
  609.6 13.0 %collective-permute-done.17 = f32[3,1,96,129]{3,2,1,0:T(8,128)S(1)} collective-permute-done((f32[3,1,96,129]{3,2,1,0:T(8,128)S(1)}, f32[3,1,96,129]{3,2,1,0:T(8,128)S(1)}, u32[]{:S(2)}, u32[]{:S(2)}) %collective-permute-start.17) | collective-permute-done | bytes 148640 | tf_op jit(solution)/shard_map/ppermute | solution.py:23
  623.7 22.1 %fusion.34 = f32[1,8,96,128]{3,2,1,0:T(8,128)S(1)} fusion(f32[1,8,96,128]{3,2,1,0:T(8,128)S(1)} %copy-done.20, f32[3,9,96,129]{3,2,1,0:T(8,128)S(1)} %pad_maximum_fusion.2, f32[3,8,96,1]{3,2,1,0:T(8,128)S(1)} %copy.114, f32[3,8,96,128]{3,2,1,0:T(8,128)S(1)} %multiply_add_fusion.1, s32[1,8,96,128]{3,2,1,0:T(8,128)S(1)} %copy-done.21), kind=kLoop, calls=%fused_computation.120 | loop fusion | flops 92110848 | bytes 9732096 | tf_op jit(solution)/shard_map/div | solution.py:238
  646.0 15.0 %all_to_all.24 = f32[1,8,96,128]{3,1,0,2:T(8,128)S(1)} all-to-all(f32[1,8,96,128]{3,1,0,2:T(8,128)S(1)} %copy.115), channel_id=1, replica_groups=mesh['gx'=8,'gy'=4,'gz'=16] {'gy'}, dimensions={2} | all-to-all | bytes 786432 | tf_op jit(solution)/shard_map/all_to_all | solution.py:205
  661.3 8.6 collective-permute-start.18
  671.9 2.8 collective-permute-done.18
  674.6 4.4 collective-permute-done.19
  682.1 10.8 %collective-permute-done.20 = f32[32,24,176]{2,1,0:T(8,128)S(1)} collective-permute-done((f32[32,24,176]{2,1,0:T(8,128)S(1)}, f32[32,24,176]{2,1,0:T(8,128)S(1)}, u32[]{:S(2)}, u32[]{:S(2)}) %collective-permute-start.20) | collective-permute-done | bytes 540704 | tf_op jit(solution)/shard_map/ppermute | solution.py:37
  692.8 21.9 %collective-permute-done.21 = f32[32,24,176]{2,1,0:T(8,128)S(1)} collective-permute-done((f32[32,24,176]{2,1,0:T(8,128)S(1)}, f32[32,24,176]{2,1,0:T(8,128)S(1)}, u32[]{:S(2)}, u32[]{:S(2)}) %collective-permute-start.21) | collective-permute-done | bytes 540704 | tf_op jit(solution)/shard_map/ppermute | solution.py:40
  715.4 4.5 collective-permute-start.22
  721.8 35.5 %collective-permute-done.22 = f32[24,72,176]{2,1,0:T(8,128)S(1)} collective-permute-done((f32[24,72,176]{2,1,0:T(8,128)S(1)}, f32[24,72,176]{2,1,0:T(8,128)S(1)}, u32[]{:S(2)}, u32[]{:S(2)}) %collective-permute-start.22) | collective-permute-done | bytes 1216544 | tf_op jit(solution)/shard_map/ppermute | solution.py:37
  757.4 4.2 collective-permute-done.23
  761.6 5.6 fusion
  772.6 4.0 all-to-all-start.1
  778.6 3.2 fusion.27
  781.8 100.2 %psum.39 = f32[]{:T(128)} all-reduce(f32[]{:T(128)} %get-tuple-element.50), channel_id=1, replica_groups=mesh['gx'=8,'gy'=4,'gz'=16] {'gx','gy','gz'}, use_global_device_ids=true, to_apply=%region_10.11 | all-reduce | flops 1 | bytes 8 | tf_op jit(solution)/shard_map/psum | solution.py:243
  (183 shorter events, 141.5 us)
Async XLA Ops:
  1.8 3.2 copy-start.2
  9.8 6.7 copy-start.17
  9.8 17.8 %collective-permute-start = (f32[3,1,96,129]{3,2,1,0:T(8,128)S(1)}, f32[3,1,96,129]{3,2,1,0:T(8,128)S(1)}, u32[]{:S(2)}, u32[]{:S(2)}) collective-permute-start(f32[3,1,96,129]{3,2,1,0:T(8,128)S(1)} %slice.538), channel_id=1, source_target_pairs={{48,0},{0,16},{16,32},{32,48},{49,1},{1,17},{17,33},{33,49},{50,2}... | collective-permute-start | bytes 445832 | tf_op jit(solution)/shard_map/ppermute | solution.py:29
  16.5 14.9 %copy-start.23 = (s32[1,8,96,128]{3,2,1,0:T(8,128)S(1)}, s32[1,8,96,128]{3,2,1,0:T(8,128)}, u32[]{:S(2)}) copy-start(s32[1,8,96,128]{3,2,1,0:T(8,128)} %param.7) | copy-start | bytes 1179652
  16.7 31.6 %copy-start = (f32[3,7,96,129]{3,2,1,0:T(8,128)}, f32[3,7,96,129]{3,2,1,0:T(8,128)S(1)}, u32[]{:S(2)}) copy-start(f32[3,7,96,129]{3,2,1,0:T(8,128)S(1)} %slice.539) | copy-start | bytes 3120772
  27.7 8.8 collective-permute-start.1
  37.5 10.8 %copy-start.18 = (f32[3,1,96,129]{3,2,1,0:T(8,128)}, f32[3,1,96,129]{3,2,1,0:T(8,128)S(1)}, u32[]{:S(2)}) copy-start(f32[3,1,96,129]{3,2,1,0:T(8,128)S(1)} %slice_add_fusion.1) | copy-start | bytes 445828
  40.2 6.6 collective-permute-start.2
  48.3 1.6 copy-start.7
  48.3 2.0 copy-start.15
  50.2 1.1 copy-start.10
  51.7 5.0 collective-permute-start.3
  59.1 21.8 %collective-permute-start.4 = (f32[3,1,96,129]{3,2,1,0:T(8,128)S(1)}, f32[3,1,96,129]{3,2,1,0:T(8,128)S(1)}, u32[]{:S(2)}, u32[]{:S(2)}) collective-permute-start(f32[3,1,96,129]{3,2,1,0:T(8,128)S(1)} %pad_maximum_fusion.19), channel_id=1, source_target_pairs={{16,0},{32,16},{48,32},{0,48},{17,1},{33,17},{49,33},{1,49},{18,2}... | collective-permute-start | bytes 445832 | tf_op jit(solution)/shard_map/ppermute | solution.py:29
  80.9 10.6 %collective-permute-start.5 = (f32[3,1,96,129]{3,2,1,0:T(8,128)S(1)}, f32[3,1,96,129]{3,2,1,0:T(8,128)}, u32[]{:S(2)}, u32[]{:S(2)}) collective-permute-start(f32[3,1,96,129]{3,2,1,0:T(8,128)S(1)} %collective-permute-done.4), channel_id=1, source_target_pairs={{1,0},{2,1},{3,2},{4,3},{5,4},{6,5},{7,6},{8,7},{9,8},{10,9},{11,1... | collective-permute-start | bytes 445832 | tf_op jit(solution)/shard_map/ppermute | solution.py:23
  91.5 1.6 copy-start.3
  128.6 16.2 %collective-permute-start.6 = (f32[3,1,96,129]{3,2,1,0:T(8,128)S(1)}, f32[3,1,96,129]{3,2,1,0:T(8,128)S(1)}, u32[]{:S(2)}, u32[]{:S(2)}) collective-permute-start(f32[3,1,96,129]{3,2,1,0:T(8,128)S(1)} %pad_maximum_fusion.18), channel_id=1, source_target_pairs={{48,0},{0,16},{16,32},{32,48},{49,1},{1,17},{17,33},{33,49},{50,2}... | collective-permute-start | bytes 445832 | tf_op jit(solution)/shard_map/ppermute | solution.py:29
  144.8 12.1 %collective-permute-start.7 = (f32[3,1,96,129]{3,2,1,0:T(8,128)S(1)}, f32[3,1,96,129]{3,2,1,0:T(8,128)S(1)}, u32[]{:S(2)}, u32[]{:S(2)}) collective-permute-start(f32[3,1,96,129]{3,2,1,0:T(8,128)S(1)} %collective-permute-done.6), channel_id=1, source_target_pairs={{0,1},{1,2},{2,3},{3,4},{4,5},{5,6},{6,7},{7,8},{8,9},{9,10},{10,1... | collective-permute-start | bytes 445832 | tf_op jit(solution)/shard_map/ppermute | solution.py:23
  157.3 1.4 copy-start.13
  159.2 8.4 collective-permute-start.8
  169.0 2.0 copy-start.8
  169.0 2.3 copy-start.16
  170.9 102.1 %copy-start.5 = (f32[3,8,96,1]{3,2,1,0:T(8,128)}, f32[3,8,96,1]{3,2,1,0:T(8,128)S(1)}, u32[]{:S(2)}) copy-start(f32[3,8,96,1]{3,2,1,0:T(8,128)S(1)} %slice_add_fusion) | copy-start | bytes 27652
  376.7 5.0 collective-permute-start.9
  383.1 27.6 %copy-start.4 = (f32[3,8,96,1]{3,2,1,0:T(8,128)S(1)}, f32[3,8,96,1]{3,2,1,0:T(8,128)}, u32[]{:S(2)}) copy-start(f32[3,8,96,1]{3,2,1,0:T(8,128)} %copy.109) | copy-start | bytes 27652
  384.1 13.6 %collective-permute-start.10 = (f32[3,1,96,129]{3,2,1,0:T(8,128)S(1)}, f32[3,1,96,129]{3,2,1,0:T(8,128)S(1)}, u32[]{:S(2)}, u32[]{:S(2)}) collective-permute-start(f32[3,1,96,129]{3,2,1,0:T(8,128)S(1)} %pad_maximum_fusion.17), channel_id=1, source_target_pairs={{16,0},{32,16},{48,32},{0,48},{17,1},{33,17},{49,33},{1,49},{18,2}... | collective-permute-start | bytes 445832 | tf_op jit(solution)/shard_map/ppermute | solution.py:29
  397.8 12.9 %collective-permute-start.11 = (f32[3,1,96,129]{3,2,1,0:T(8,128)S(1)}, f32[3,1,96,129]{3,2,1,0:T(8,128)S(1)}, u32[]{:S(2)}, u32[]{:S(2)}) collective-permute-start(f32[3,1,96,129]{3,2,1,0:T(8,128)S(1)} %collective-permute-done.10), channel_id=1, source_target_pairs={{1,0},{2,1},{3,2},{4,3},{5,4},{6,5},{7,6},{8,7},{9,8},{10,9},{11,1... | collective-permute-start | bytes 445832 | tf_op jit(solution)/shard_map/ppermute | solution.py:23
  446.7 11.7 %collective-permute-start.12 = (f32[3,1,96,129]{3,2,1,0:T(8,128)S(1)}, f32[3,1,96,129]{3,2,1,0:T(8,128)S(1)}, u32[]{:S(2)}, u32[]{:S(2)}) collective-permute-start(f32[3,1,96,129]{3,2,1,0:T(8,128)S(1)} %pad_maximum_fusion.16), channel_id=1, source_target_pairs={{48,0},{0,16},{16,32},{32,48},{49,1},{1,17},{17,33},{33,49},{50,2}... | collective-permute-start | bytes 445832 | tf_op jit(solution)/shard_map/ppermute | solution.py:29
  458.4 7.5 collective-permute-start.13
  466.2 1.8 copy-start.14
  468.3 11.1 %collective-permute-start.14 = (f32[3,8,96,1]{2,1,3,0:T(8,128)S(1)}, f32[3,8,96,1]{2,1,3,0:T(8,128)S(1)}, u32[]{:S(2)}, u32[]{:S(2)}) collective-permute-start(f32[3,8,96,1]{2,1,3,0:T(8,128)S(1)} %copy.110), channel_id=1, source_target_pairs={{0,64},{64,128},{128,192},{192,256},{256,320},{320,384},{384,448},... | collective-permute-start | bytes 27656 | tf_op jit(solution)/shard_map/ppermute | solution.py:23
  477.7 3.2 copy-start.12
  590.8 5.6 collective-permute-start.15
  596.8 11.5 %collective-permute-start.16 = (f32[3,1,96,129]{3,2,1,0:T(8,128)S(1)}, f32[3,1,96,129]{3,2,1,0:T(8,128)S(1)}, u32[]{:S(2)}, u32[]{:S(2)}) collective-permute-start(f32[3,1,96,129]{3,2,1,0:T(8,128)S(1)} %pad_maximum_fusion.15), channel_id=1, source_target_pairs={{16,0},{32,16},{48,32},{0,48},{17,1},{33,17},{49,33},{1,49},{18,2}... | collective-permute-start | bytes 445832 | tf_op jit(solution)/shard_map/ppermute | solution.py:29
  608.3 14.3 %collective-permute-start.17 = (f32[3,1,96,129]{3,2,1,0:T(8,128)S(1)}, f32[3,1,96,129]{3,2,1,0:T(8,128)S(1)}, u32[]{:S(2)}, u32[]{:S(2)}) collective-permute-start(f32[3,1,96,129]{3,2,1,0:T(8,128)S(1)} %collective-permute-done.16), channel_id=1, source_target_pairs={{1,0},{2,1},{3,2},{4,3},{5,4},{6,5},{7,6},{8,7},{9,8},{10,9},{11,1... | collective-permute-start | bytes 445832 | tf_op jit(solution)/shard_map/ppermute | solution.py:23
  622.6 1.1 copy-start.21
  661.3 13.3 %collective-permute-start.18 = (f32[32,24,24]{2,1,0:T(8,128)S(1)}, f32[32,24,24]{2,1,0:T(8,128)S(1)}, u32[]{:S(2)}, u32[]{:S(2)}) collective-permute-start(f32[32,24,24]{2,1,0:T(8,128)S(1)} %get-tuple-element.40), channel_id=1, source_target_pairs={{0,64},{64,128},{128,192},{192,256},{256,320},{320,384},{384,448},... | collective-permute-start | bytes 221192 | tf_op jit(solution)/shard_map/ppermute | solution.py:37
  669.9 9.1 %collective-permute-start.19 = (f32[32,24,24]{2,1,0:T(8,128)S(1)}, f32[32,24,24]{2,1,0:T(8,128)S(1)}, u32[]{:S(2)}, u32[]{:S(2)}) collective-permute-start(f32[32,24,24]{2,1,0:T(8,128)S(1)} %get-tuple-element.41), channel_id=1, source_target_pairs={{64,0},{128,64},{192,128},{256,192},{320,256},{384,320},{448,384},... | collective-permute-start | bytes 221192 | tf_op jit(solution)/shard_map/ppermute | solution.py:40
  679.4 13.4 %collective-permute-start.20 = (f32[32,24,176]{2,1,0:T(8,128)S(1)}, f32[32,24,176]{2,1,0:T(8,128)S(1)}, u32[]{:S(2)}, u32[]{:S(2)}) collective-permute-start(f32[32,24,176]{2,1,0:T(8,128)S(1)} %pad_maximum_fusion.5), channel_id=1, source_target_pairs={{0,16},{16,32},{32,48},{1,17},{17,33},{33,49},{2,18},{18,34},{34,5... | collective-permute-start | bytes 1622024 | tf_op jit(solution)/shard_map/ppermute | solution.py:37
  680.8 33.9 %collective-permute-start.21 = (f32[32,24,176]{2,1,0:T(8,128)S(1)}, f32[32,24,176]{2,1,0:T(8,128)S(1)}, u32[]{:S(2)}, u32[]{:S(2)}) collective-permute-start(f32[32,24,176]{2,1,0:T(8,128)S(1)} %pad_maximum_fusion.5), channel_id=1, source_target_pairs={{16,0},{32,16},{48,32},{17,1},{33,17},{49,33},{18,2},{34,18},{50,3... | collective-permute-start | bytes 1622024 | tf_op jit(solution)/shard_map/ppermute | solution.py:40
  715.4 42.0 %collective-permute-start.22 = (f32[24,72,176]{2,1,0:T(8,128)S(1)}, f32[24,72,176]{2,1,0:T(8,128)S(1)}, u32[]{:S(2)}, u32[]{:S(2)}) collective-permute-start(f32[24,72,176]{2,1,0:T(8,128)S(1)} %get-tuple-element.36), channel_id=1, source_target_pairs={{0,1},{1,2},{2,3},{3,4},{4,5},{5,6},{6,7},{7,8},{8,9},{9,10},{10,1... | collective-permute-start | bytes 3649544 | tf_op jit(solution)/shard_map/ppermute | solution.py:37
  719.9 41.7 %collective-permute-start.23 = (f32[24,72,176]{2,1,0:T(8,128)S(1)}, f32[24,72,176]{2,1,0:T(8,128)S(1)}, u32[]{:S(2)}, u32[]{:S(2)}) collective-permute-start(f32[24,72,176]{2,1,0:T(8,128)S(1)} %get-tuple-element.37), channel_id=1, source_target_pairs={{1,0},{2,1},{3,2},{4,3},{5,4},{6,5},{7,6},{8,7},{9,8},{10,9},{11,1... | collective-permute-start | bytes 3649544 | tf_op jit(solution)/shard_map/ppermute | solution.py:40
  769.4 7.2 copy-start.1
  769.4 7.2 copy-start.19
  772.6 110.0 %all-to-all-start.1 = ((f32[1,32,24,128]{3,2,0,1:T(8,128)}), f32[1,32,24,128]{3,2,0,1:T(8,128)S(1)}, u32[]{:S(2)}, u32[]{:S(2)}) async-start(f32[1,32,24,128]{3,2,0,1:T(8,128)} %copy.119), calls=%async_computation.1 | async-start | bytes 786432 | tf_op jit(solution)/shard_map/all_to_all | solution.py:209
  776.6 1.3 copy-start.6
  776.6 1.6 copy-start.9
  776.6 2.0 copy-start.11
  781.8 100.9 %copy-start.22 = (s32[1,8,96,128]{3,2,1,0:T(8,128)S(1)}, s32[1,8,96,128]{3,2,1,0:T(8,128)}, u32[]{:S(2)}) copy-start(s32[1,8,96,128]{3,2,1,0:T(8,128)} %param.6) | copy-start | bytes 1179652
  (1 other events, 1.0 us)
where the time goes:
time: 890 us; the launch traced here: 884 us
  blocking collectives  414 us (47%)
  waiting for transfers between devices  197 us (22%)
  other arithmetic  128 us (14%)
  starting transfers between devices  96.2 us (11%)
  local copies, waits for them, and re-layouts  32.1 us (4%)
  matrix products  10 us (1%)
    psum x2, blocking collectives, inner_sum(): return lax.psum(jnp.sum(values), ('gx', 'gy', 'gz'))  195 us
    psum x1, blocking collectives, on_device(): alpha = gamma / lax.psum(jnp.sum(search * image), ('gx', 'gy', 'gz'))  104 us
    psum x1, blocking collectives, on_device(): total = lax.psum(jnp.sum(stimulus), ('gx', 'gy', 'gz'))  100 us
    mul x48, other arithmetic, lean_forces(): term = moduli * products[component * 8 + node]  65.4 us
    ppermute x6, waiting for transfers between devices, from_behind(): return lax.ppermute(block, axis, route)  61.3 us
    ppermute x12, waiting for transfers between devices, shifted(): lax.ppermute(value, axis, [(source, source + steps) for source in range(i...  56.6 us
    ppermute x3, waiting for transfers between devices, extended(): lax.ppermute(lax.slice_in_dim(block, block.shape[dim] - width, None, axis...  49 us
    ppermute x12, starting transfers between devices, shifted(): lax.ppermute(value, axis, [(source, source + steps) for source in range(i...  42.1 us
  transfers between devices with their start and end apart: 25, of which 21 were waited for; matrix products, arithmetic and copies ran while one was open for 1% of the time, Pallas kernels for 0%

commit v1 on v0

v1 whole, which is shorter than its diff:
```python
import functools
import math

import jax
import jax.numpy as jnp
import numpy as np
from jax import lax
from jax.experimental import pallas as pl
from jax.experimental.pallas import tpu as pltpu
from jax.sharding import PartitionSpec as P

MESH = pl.DeviceIdType.MESH
RAD = 24
MARROW = 0.1
REMODEL = 0.25
FLOOR = 0.2
CEILING = 1.0
EPSILON = 1e-06
DEP = 8
HEI = 96
WID = 128
F32 = jnp.float32
BF16 = jnp.bfloat16


def element_stiffness():
    poisson = 0.3
    lame = poisson / ((1.0 + poisson) * (1.0 - 2.0 * poisson))
    shear = 0.5 / (1.0 + poisson)
    elastic = np.zeros((6, 6))
    elastic[:3, :3] = lame
    for index in range(3):
        elastic[index, index] += 2.0 * shear
        elastic[index + 3, index + 3] = shear
    points = [0.5 - 0.5 / math.sqrt(3.0), 0.5 + 0.5 / math.sqrt(3.0)]
    matrix = np.zeros((24, 24))
    for point_z in points:
        for point_y in points:
            for point_x in points:
                strain = np.zeros((6, 24))
                for corner_z in range(2):
                    for corner_y in range(2):
                        for corner_x in range(2):
                            node = 4 * corner_z + 2 * corner_y + corner_x
                            shape_x = point_x if corner_x else 1.0 - point_x
                            shape_y = point_y if corner_y else 1.0 - point_y
                            shape_z = point_z if corner_z else 1.0 - point_z
                            slope_x = 1.0 if corner_x else -1.0
                            slope_y = 1.0 if corner_y else -1.0
                            slope_z = 1.0 if corner_z else -1.0
                            along_x = slope_x * shape_y * shape_z
                            along_y = shape_x * slope_y * shape_z
                            along_z = shape_x * shape_y * slope_z
                            strain[0, node] = along_x
                            strain[1, 8 + node] = along_y
                            strain[2, 16 + node] = along_z
                            strain[3, node] = along_y
                            strain[3, 8 + node] = along_x
                            strain[4, 8 + node] = along_z
                            strain[4, 16 + node] = along_y
                            strain[5, node] = along_z
                            strain[5, 16 + node] = along_x
                matrix = matrix + strain.T @ elastic @ strain / 8.0
    return matrix


KE = element_stiffness()
HAAR1 = np.array([[1.0, 1.0], [-1.0, 1.0]])
HAAR = np.kron(np.eye(3), np.kron(HAAR1, np.kron(HAAR1, HAAR1)))
KH = HAAR @ KE @ HAAR.T / 64.0
DIAG = float(KE[0, 0])
GROUPS = ((1, 10, 20), (2, 9), (4, 17), (12, 18), (3, 22), (5, 14), (11, 21), (6, 13, 19), (7,), (15,), (23,))
LAMBDA = math.exp(-1.0 / 12.0)
NORMAL = 1.0 / (1.0 + 2.0 * sum(LAMBDA**d for d in range(1, RAD + 1)))


def stress(m):
    out = [None] * 24
    for group in GROUPS:
        first = group[0]
        diag = float(KH[first, first])
        if len(group) == 1:
            out[first] = diag * m[first]
            continue
        off = float(KH[first, group[1]])
        total = m[first]
        for k in group[1:]:
            total = total + m[k]
        common = off * total
        for k in group:
            out[k] = common if abs(diag - off) < 1e-12 else common + (diag - off) * m[k]
    return out


def bilinear(m, f):
    total = None
    for k in range(24):
        if f[k] is not None:
            total = m[k] * f[k] if total is None else total + m[k] * f[k]
    return total


def zmodes(lo, hi):
    m = [None] * 24
    for c in range(3):
        for p in range(4):
            m[c * 8 + p] = hi[c * 4 + p] + lo[c * 4 + p]
            m[c * 8 + 4 + p] = hi[c * 4 + p] - lo[c * 4 + p]
    return m


def minus(a, b):
    return -b if a is None else a - b


def plus(a, b):
    return b if a is None else a + b


def split(value):
    hi = value.astype(BF16)
    return hi, (value - hi.astype(F32)).astype(BF16)


def dot(a, b):
    return jnp.dot(a, b, preferred_element_type=F32)


def body(sizes, dens, bone, fixed, load, out_d, out_u, s):
    GX, GY, GZ = sizes
    S = GY * GZ
    gx, gy, gz = lax.axis_index("gx"), lax.axis_index("gy"), lax.axis_index("gz")
    slab = gz * GY + gy
    lane = lax.broadcasted_iota(jnp.int32, (HEI, WID), 1)
    rowi = lax.broadcasted_iota(jnp.int32, (HEI, WID), 0)

    def device(dx=0, ds=0):
        t = lax.rem(slab + ds + S, S)
        return (lax.rem(gx + dx + GX, GX), lax.rem(t, GY), lax.div(t, GY))

    def flag(cond):
        return jnp.where(cond, 1.0, 0.0).astype(F32)

    has_left, has_right = flag(gx > 0), flag(gx < GX - 1)
    has_down, has_up = flag(slab > 0), flag(slab < S - 1)

    count = [0]
    sends = []

    def remote(src, dst, target):
        k = count[0]
        count[0] += 1
        copy = pltpu.make_async_remote_copy(
            src_ref=src, dst_ref=dst, send_sem=s["send"].at[k], recv_sem=s["recv"].at[k],
            device_id=target, device_id_type=MESH)
        copy.start()
        sends.append(copy)
        return copy

    barrier = pltpu.get_barrier_semaphore()
    peers = [device(-1), device(1), device(0, 1), device(0, -1), device(0, 3), device(0, -3),
             device(1, 1), device(-1, -1), device(-1, 1), device(1, -1)]
    for k in range(1, GX):
        peers.append((lax.rem(gx + k, GX), gy, gz))
    for k in range(1, GY):
        peers.append((gx, lax.rem(gy + k, GY), gz))
    for k in range(1, GZ):
        peers.append((gx, gy, lax.rem(gz + k, GZ)))
    for peer in peers:
        pl.semaphore_signal(barrier, inc=1, device_id=peer, device_id_type=MESH)

    E, R = s["E"], s["R"]

    @pl.loop(0, DEP)
    def _(z):
        b = bone[0, z].astype(F32)
        d = dens[0, z]
        E[z + 1] = b * d * d + (1.0 - b) * MARROW
        f = 1.0 - fixed[0, z].astype(F32)
        for c in range(3):
            R[c, z] = f * load[c, 0, z]

    zero8 = jnp.zeros((8, WID), F32)

    @pl.loop(0, 10)
    def _(zz):
        for k in range(6):
            s["SDs"][k, zz, pl.ds(HEI, 8)] = zero8
            s["SDw"][k, zz, pl.ds(HEI, 8)] = zero8
            s["B"][k, zz, pl.ds(0, 8)] = zero8

    for k in range(6):
        s["XSD"][k, pl.ds(HEI, 8)] = zero8
    for k in range(3):
        s["XB"][k, pl.ds(0, 8)] = zero8

    def pack(get, slots, src):
        acc = jnp.zeros((HEI, WID), F32)
        for index, k in slots:
            acc = jnp.where(lane == k, pltpu.roll(get(index), (k - src) % WID, 1), acc)
        return acc

    def turned(acc):
        full = jnp.concatenate([acc, jnp.zeros((WID - HEI, WID), F32)], axis=0)
        return jnp.transpose(full)

    def unturned(ref, rows):
        got = ref[...]
        full = jnp.concatenate([got, jnp.zeros((WID - rows, WID), F32)], axis=0) if rows < WID else got
        return jnp.transpose(full)[:HEI]

    s["XEs"][...] = turned(pack(lambda z: E[z + 1], [(z, z) for z in range(DEP)], WID - 1))[:8]

    pl.semaphore_wait(barrier, len(peers))
    c_xe = remote(s["XEs"], s["XEr"], device(1))
    c_xd = remote(s["XEs"], s["XDr"], device(1, 1))
    c_r = remote(R.at[:, 0], s["R8"], device(0, -1))
    c_e = remote(E.at[DEP], E.at[0], device(0, 1))

    far_y = jnp.abs(lax.broadcasted_iota(jnp.int32, (HEI, HEI), 0) - lax.broadcasted_iota(jnp.int32, (HEI, HEI), 1))
    s["Wy"][0], s["Wy"][1] = split(tap(far_y))
    row = lax.broadcasted_iota(jnp.int32, (WID, WID), 0)
    col = lax.broadcasted_iota(jnp.int32, (WID, WID), 1)
    s["Wx"][0, 0], s["Wx"][0, 1] = split(tap(jnp.abs(row - col)))
    for j in range(4):
        inside = (row >= 32 * j) & (row < 32 * j + 32)
        right = jnp.where(inside, tap(jnp.abs(WID + row - 32 * j - col)), 0.0)
        left = jnp.where(inside, tap(jnp.abs(col + 32 - row + 32 * j)), 0.0)
        s["Wx"][1 + j, 0], s["Wx"][1 + j, 1] = split(left)
        s["Wx"][5 + j, 0], s["Wx"][5 + j, 1] = split(right)

    T = s["T"]

    def inplane(e, edge):
        ex = e + jnp.where(lane == 0, edge, pltpu.roll(e, 1, 1))
        return ex + jnp.where(rowi == 0, 0.0, pltpu.roll(ex, 1, 0))

    c_xe.wait_recv()
    s["XE"][...] = unturned(s["XEr"], 8) * has_left

    @pl.loop(0, DEP)
    def _(z):
        T[z + 1] = inplane(E[z + 1], pltpu.roll(s["XE"][...], lax.rem(WID - z, WID), 1))

    c_t = remote(T.at[1], T.at[DEP + 1], device(0, -1))
    s0, Q = s["s0"], s["Q"]

    def start(z):
        inv = 1.0 / (DIAG * (T[z] + T[z + 1]))
        Q[z] = (1.0 - fixed[0, z].astype(F32)) * inv
        for c in range(3):
            s0[c, z + 1] = R[c, z] * inv

    start(DEP - 1)
    c_s = remote(s0.at[:, DEP], s0.at[:, 0], device(0, 1))
    pl.loop(1, DEP - 1)(start)

    c_xd.wait_recv()
    c_e.wait_recv()
    E[0] = E[0] * has_down
    xd = unturned(s["XDr"], 8) * (has_left * has_down)
    T[0] = inplane(E[0], pltpu.roll(xd, WID - 7, 1))
    start(0)
    s["EX"][...] = jnp.where(lane == 0, pltpu.roll(xd, WID - 7, 1), pltpu.roll(s["XE"][...], 1, 1))

    c_r.wait_recv()
    c_t.wait_recv()
    inv8 = has_up / (DIAG * (T[DEP] + has_up * T[DEP + 1]))
    for c in range(3):
        s0[c, DEP + 1] = s["R8"][c] * inv8
    c_s.wait_recv()

    slots = [((c, zz), 16 * c + zz) for c in range(3) for zz in range(10)]
    first = pack(lambda i: s0[i[0], i[1]], slots, 0)
    last = pack(lambda i: s0[i[0], i[1]], slots, WID - 1)
    s["X0"][...] = first
    s["XLs"][...] = turned(first)[:48]
    s["XRs"][...] = turned(last)[:48]
    c_xl = remote(s["XLs"], s["XRr"], device(-1))
    c_xr = remote(s["XRs"], s["XLr"], device(1))
    c_xl.wait_recv()
    c_xr.wait_recv()
    s["XH"][...] = unturned(s["XRr"], 48) * has_right
    xl = unturned(s["XLr"], 48)
    for c in range(3):
        s["XSD"][2 * c, pl.ds(0, HEI)] = pltpu.roll(s["X0"][...] + xl, (WID - 16 * c) % WID, 1)
        s["XSD"][2 * c + 1, pl.ds(0, HEI)] = pltpu.roll(s["X0"][...] - xl, (WID - 16 * c) % WID, 1)

    def xstage(field, SD, halo, zz):
        for c in range(3):
            v = field[c, zz]
            h = pltpu.roll(halo[...], WID - 1 - 16 * c - zz, 1)
            v1 = jnp.where(lane == WID - 1, h, pltpu.roll(v, WID - 1, 1))
            SD[2 * c, zz, pl.ds(0, HEI)] = v1 + v
            SD[2 * c + 1, zz, pl.ds(0, HEI)] = v1 - v

    pl.loop(0, 10)(lambda zz: xstage(s0, s["SDs"], s["XH"], zz))

    def planar(SD, zz, y0):
        out = []
        for c in range(3):
            a0, a1 = SD[2 * c, zz, pl.ds(y0, 8)], SD[2 * c, zz, pl.ds(y0 + 1, 8)]
            b0, b1 = SD[2 * c + 1, zz, pl.ds(y0, 8)], SD[2 * c + 1, zz, pl.ds(y0 + 1, 8)]
            out += [a1 + a0, b1 + b0, a1 - a0, b1 - b0]
        return out

    A, B = s["A"], s["B"]

    @pl.loop(0, HEI // 8)
    def _(i):
        y0 = pl.multiple_of(i * 8, 8)

        def plane(zz, carry):
            lo, above = carry
            hi = planar(s["SDs"], zz + 1, y0)
            f = stress(zmodes(lo, hi))
            e = E[zz, pl.ds(y0, 8)]
            f = [None if v is None else v * e for v in f]
            up = [plus(f[c * 8 + p], f[c * 8 + 4 + p]) for c in range(3) for p in range(4)]
            down = [minus(f[c * 8 + p], f[c * 8 + 4 + p]) for c in range(3) for p in range(4)]
            g = [u + v for u, v in zip(above, down)]
            for c in range(3):
                for ix in range(2):
                    A[2 * c + ix, zz, pl.ds(y0, 8)] = g[4 * c + ix] - g[4 * c + 2 + ix]
                    B[2 * c + ix, zz, pl.ds(y0 + 8, 8)] = g[4 * c + ix] + g[4 * c + 2 + ix]
            return tuple(hi), tuple(up)

        z8 = jnp.zeros((8, WID), F32)
        lax.fori_loop(0, DEP + 1, plane, (tuple(planar(s["SDs"], 0, y0)), (z8,) * 12))
        lo = []
        for c in range(3):
            a0, a1 = s["XSD"][2 * c, pl.ds(y0, 8)], s["XSD"][2 * c, pl.ds(y0 + 1, 8)]
            b0, b1 = s["XSD"][2 * c + 1, pl.ds(y0, 8)], s["XSD"][2 * c + 1, pl.ds(y0 + 1, 8)]
            lo += [a1 + a0, b1 + b0, a1 - a0, b1 - b0]
        hi = [pltpu.roll(v, WID - 1, 1) for v in lo]
        f = stress(zmodes(lo, hi))
        e = s["EX"][pl.ds(y0, 8)]
        f = [None if v is None else v * e for v in f]
        for c in range(3):
            g = []
            for p in range(4):
                up = plus(f[c * 8 + p], f[c * 8 + 4 + p])
                down = minus(f[c * 8 + p], f[c * 8 + 4 + p])
                g.append(down + pltpu.roll(up, 1, 1))
            s["XA"][c, pl.ds(y0, 8)] = (g[0] - g[2]) + (g[1] - g[3])
            s["XB"][c, pl.ds(y0 + 8, 8)] = (g[0] + g[2]) + (g[1] + g[3])

    for c in range(3):
        s["XF"][c] = s["XA"][c] + s["XB"][c, pl.ds(7, HEI)]

    w0 = s["w0"]

    def image(z, sums):
        gamma, delta, eps = sums
        q = Q[z]
        for c in range(3):
            gs = A[2 * c, z + 1] + B[2 * c, z + 1, pl.ds(7, HEI)]
            gd = A[2 * c + 1, z + 1] + B[2 * c + 1, z + 1, pl.ds(7, HEI)]
            edge = pltpu.roll(s["XF"][c], WID - 1 - z, 1)
            im = (gs - gd) + jnp.where(lane == 0, edge, pltpu.roll(gs + gd, 1, 1))
            w = im * q
            w0[c, z] = w
            v = s0[c, z + 1]
            gamma = gamma + R[c, z] * v
            delta = delta + v * im
            eps = eps + w * im
        return gamma, delta, eps

    zp = jnp.zeros((HEI, WID), F32)
    sums = image(0, (zp, zp, zp))
    c_w = remote(w0.at[:, 0], w0.at[:, DEP], device(0, -1))
    sums = lax.fori_loop(1, DEP, image, sums)

    slots = [((c, z), 8 * z + c) for z in range(DEP) for c in range(3)]
    s["XWs"][...] = turned(pack(lambda i: w0[i[0], i[1]], slots, 0))[:64]
    c_xw = remote(s["XWs"], s["XWr"].at[pl.ds(0, 64)], device(-1))
    c_xc = remote(s["XWs"].at[pl.ds(0, 8)], s["XCr"], device(-1, -1))

    SDs, SDw, SE = s["SDs"], s["SDw"], s["SE"]

    def chunks(step):
        @pl.loop(0, HEI // 8)
        def _(i):
            step(pl.multiple_of(i * 8, 8))

    def self_energy(y0):
        def plane(z, lo):
            hi = planar(SDs, z + 2, y0)
            m = zmodes(lo, hi)
            SE[0, z, pl.ds(y0, 8)] = bilinear(m, stress(m))
            return tuple(hi)
        lax.fori_loop(0, DEP, plane, tuple(planar(SDs, 1, y0)))

    chunks(self_energy)

    c_xw.wait_recv()
    c_xc.wait_recv()
    s["XWr"][pl.ds(64, 8)] = s["XCr"][...] * has_up
    s["XH"][...] = unturned(s["XWr"], 72) * has_right
    c_w.wait_recv()
    for c in range(3):
        w0[c, DEP] = w0[c, DEP] * has_up

    @pl.loop(0, DEP + 1)
    def _(z):
        for c in range(3):
            v = w0[c, z]
            h = pltpu.roll(s["XH"][...], WID - 1 - 8 * z - c, 1)
            v1 = jnp.where(lane == WID - 1, h, pltpu.roll(v, WID - 1, 1))
            SDw[2 * c, z, pl.ds(0, HEI)] = v1 + v
            SDw[2 * c + 1, z, pl.ds(0, HEI)] = v1 - v

    def w_energy(i, zeta):
        y0 = pl.multiple_of(i * 8, 8)

        def plane(z, carry):
            lo, total = carry
            hi = planar(SDw, z + 1, y0)
            m = zmodes(lo, hi)
            q = bilinear(m, stress(m))
            SE[2, z, pl.ds(y0, 8)] = q
            return tuple(hi), total + q * E[z + 1, pl.ds(y0, 8)]
        return lax.fori_loop(0, DEP, plane, (tuple(planar(SDw, 0, y0)), zeta))[1]

    zeta = lax.fori_loop(0, HEI // 8, w_energy, jnp.zeros((8, WID), F32))

    def rows(value):
        return jnp.sum(value, axis=0, keepdims=True)

    def spread(which, axis, n, me, target):
        buf = s["red"].at[which]
        copies = []
        for k in range(1, n):
            peer = lax.rem(me + k, n)
            copies.append(remote(s["own"].at[which], buf.at[me], target(peer)))
        return copies

    def gather(which, n, me, copies):
        for copy in copies:
            copy.wait_recv()
        buf = s["red"]
        buf[which, me] = s["own"][which]
        total = buf[which, 0]
        for k in range(1, n):
            total = total + buf[which, k]
        return total

    axes = ((GX, gx, lambda p: (p, gy, gz)), (GY, gy, lambda p: (gx, p, gz)), (GZ, gz, lambda p: (gx, gy, p)))

    def reduce_start(base, stage):
        n, me, target = axes[stage]
        return spread(base + stage, None, n, me, target)

    def reduce_end(base, stage, copies):
        n, me, _ = axes[stage]
        return gather(base + stage, n, me, copies)

    gamma, delta, eps = sums
    pad = jnp.zeros((4, WID), F32)
    s["own"][0] = jnp.concatenate([rows(gamma), rows(delta), rows(eps), rows(zeta), pad], axis=0)
    copies = reduce_start(0, 0)

    def cross_energy(y0):
        def plane(z, carry):
            los, low = carry
            his, hiw = planar(SDs, z + 2, y0), planar(SDw, z + 1, y0)
            SE[1, z, pl.ds(y0, 8)] = bilinear(zmodes(low, hiw), stress(zmodes(los, his)))
            return tuple(his), tuple(hiw)
        lax.fori_loop(0, DEP, plane, (tuple(planar(SDs, 1, y0)), tuple(planar(SDw, 0, y0))))

    chunks(cross_energy)

    s["own"][1] = reduce_end(0, 0, copies)
    copies = reduce_start(0, 1)
    s["own"][2] = reduce_end(0, 1, copies)
    copies = reduce_start(0, 2)
    total = jnp.sum(reduce_end(0, 2, copies), axis=1, keepdims=True)
    g0, d0, ep, ze = total[0:1], total[1:2], total[2:3], total[3:4]
    alpha = g0 / d0
    g1 = g0 - 2.0 * alpha * d0 + alpha * alpha * ep
    beta = g1 / g0
    d1 = (1.0 + beta) * (1.0 + beta) * d0 - 2.0 * alpha * (1.0 + beta) * ep + alpha * alpha * ze
    alpha1 = g1 / d1
    ca = jnp.broadcast_to(alpha + alpha1 * (1.0 + beta), (HEI, WID))
    cb = jnp.broadcast_to(-(alpha1 * alpha), (HEI, WID))

    G = s["G"]

    @pl.loop(0, DEP)
    def _(z):
        form = ca * ca * SE[0, z] + 2.0 * (ca * cb) * SE[1, z] + cb * cb * SE[2, z]
        G[z] = form * (0.5 * E[z + 1]) / dens[0, z]

    for b in range(2):
        acc_l = acc_r = None
        for j in range(4):
            v = G[4 * b + j]
            mine = (lane >= 32 * j) & (lane < 32 * j + 32)
            to_l = pltpu.roll(v, 32 * j, 1) if j else v
            to_r = pltpu.roll(v, (32 * j - 96) % WID, 1) if (32 * j - 96) % WID else v
            acc_l = to_l if acc_l is None else jnp.where(mine, to_l, acc_l)
            acc_r = to_r if acc_r is None else jnp.where(mine, to_r, acc_r)
        s["HLs"][b] = acc_l
        s["HRs"][b] = acc_r
    c_hl = remote(s["HLs"], s["HRr"], device(-1))
    c_hr = remote(s["HRs"], s["HLr"], device(1))

    def smooth_y(v):
        hi, lo = split(v)
        return dot(s["Wy"][0], hi) + dot(s["Wy"][1], hi) + dot(s["Wy"][0], lo)

    def smooth_x(v, k):
        hi, lo = split(v)
        return dot(hi, s["Wx"][k, 0]) + dot(hi, s["Wx"][k, 1]) + dot(lo, s["Wx"][k, 0])

    @pl.loop(0, DEP)
    def _(z):
        G[z] = smooth_x(smooth_y(G[z]), 0)

    @pl.loop(0, DEP)
    def _(z):
        for c in range(3):
            out_u[c, 0, z] = ca * s0[c, z + 1] + cb * w0[c, z]

    c_hl.wait_recv()
    c_hr.wait_recv()
    for b in range(2):
        s["HLr"][b] = smooth_y(s["HLr"][b] * has_left)
        s["HRr"][b] = smooth_y(s["HRr"][b] * has_right)

    Gup, Gdn = s["Gup"], s["Gdn"]
    planes = [None] * DEP
    order = [0, 7, 1, 6, 2, 5, 3, 4]
    for z in order:
        b, j = z // 4, z % 4
        G[z] = G[z] + smooth_x(s["HLr"][b], 1 + j) + smooth_x(s["HRr"][b], 5 + j)
        planes[z] = (remote(G.at[z], Gup.at[z], device(0, -3)), remote(G.at[z], Gdn.at[z], device(0, 3)))

    low = G[0]
    high = G[DEP - 1]
    for k in range(1, DEP):
        low = low + (LAMBDA**k) * G[k]
        high = high + (LAMBDA**k) * G[DEP - 1 - k]
    s["RU"][0] = low
    s["RD"][0] = high
    c_u0 = remote(s["RU"].at[0], s["RU"].at[1], device(0, -1))
    c_d0 = remote(s["RD"].at[0], s["RD"].at[1], device(0, 1))

    share = jnp.zeros((HEI, WID), F32)
    one = jnp.ones((HEI, WID), F32)
    for z in range(DEP):
        below = jnp.minimum(slab * DEP + z, RAD)
        above = jnp.minimum(S * DEP - 1 - slab * DEP - z, RAD)
        tail = power(one * (below + 1).astype(F32)) + power(one * (above + 1).astype(F32))
        weight = NORMAL * (1.0 + (2.0 * LAMBDA - tail) * (1.0 / (1.0 - LAMBDA)))
        share = share + weight * G[z]
    s["own"][3] = jnp.concatenate([rows(share), jnp.zeros((7, WID), F32)], axis=0)
    copies = reduce_start(3, 0)

    c_u0.wait_recv()
    c_d0.wait_recv()
    at1, at2 = flag(slab + 1 < S), flag(slab + 2 < S)
    bt1, bt2 = flag(slab - 1 >= 0), flag(slab - 2 >= 0)
    at3, bt3 = flag(slab + 3 < S), flag(slab - 3 >= 0)
    s["RU"][2] = low + LAMBDA**DEP * (at1 * s["RU"][1])
    s["RD"][2] = high + LAMBDA**DEP * (bt1 * s["RD"][1])
    c_u1 = remote(s["RU"].at[2], s["RU"].at[3], device(0, -1))
    c_d1 = remote(s["RD"].at[2], s["RD"].at[3], device(0, 1))

    s["own"][4] = reduce_end(3, 0, copies)
    copies = reduce_start(3, 1)
    F = s["F"]
    acc = jnp.zeros((HEI, WID), F32)
    for z in range(DEP):
        acc = G[z] if z == 0 else LAMBDA * acc + G[z]
        F[z] = acc
    acc = jnp.zeros((HEI, WID), F32)
    for z in range(DEP - 2, -1, -1):
        acc = LAMBDA * (acc + G[z + 1])
        F[z] = F[z] + acc
    s["own"][5] = reduce_end(3, 1, copies)
    copies = reduce_start(3, 2)
    c_u1.wait_recv()
    c_d1.wait_recv()
    near_u, near_d = at1 * s["RU"][3], bt1 * s["RD"][3]
    for z in range(DEP):
        F[z] = F[z] + LAMBDA ** (DEP - z) * near_u + LAMBDA ** (z + 1) * near_d

    mean = jnp.sum(reduce_end(3, 2, copies)[0:1], axis=1, keepdims=True)
    mean = mean / float(S * DEP * HEI * WID * GX)
    scale = NORMAL * jnp.broadcast_to(1.0 / (mean + EPSILON), (HEI, WID))

    for z in order:
        planes[z][0].wait_recv()
        planes[z][1].wait_recv()
    run = None
    for z in range(DEP):
        g = (at3 * LAMBDA**RAD) * Gup[z]
        run = g if run is None else g + (1.0 / LAMBDA) * run
        F[z] = F[z] + run
    run = None
    for z in range(DEP - 1, -1, -1):
        g = (bt3 * LAMBDA**RAD) * Gdn[z]
        run = g if run is None else g + (1.0 / LAMBDA) * run
        b = bone[0, z].astype(F32)
        new = dens[0, z] + REMODEL * b * ((F[z] + run) * scale - 1.0)
        out_d[0, z] = jnp.clip(new, FLOOR, CEILING)

    for copy in sends:
        copy.wait_send()


def tap(distance):
    return jnp.where(distance <= RAD, NORMAL * jnp.exp(distance.astype(F32) * (-1.0 / 12.0)), 0.0)


def power(exponent):
    return jnp.exp(exponent * (-1.0 / 12.0))


def on_device(sizes, density, bone, fixed, load):
    GX, GY, GZ = sizes
    copies = 4 + 2 + 2 + 3 + 2 * (GX + GY + GZ - 3) + 2 + 16 + 4
    V = pltpu.VMEM
    big = max(sizes)
    scratch = {
        "send": pltpu.SemaphoreType.DMA((copies,)),
        "recv": pltpu.SemaphoreType.DMA((copies,)),
        "E": V((9, HEI, WID), F32), "R": V((3, DEP, HEI, WID), F32), "R8": V((3, HEI, WID), F32),
        "T": V((10, HEI, WID), F32), "Q": V((DEP, HEI, WID), F32),
        "s0": V((3, 10, HEI, WID), F32), "w0": V((3, 9, HEI, WID), F32),
        "SDs": V((6, 10, HEI + 8, WID), F32), "SDw": V((6, 10, HEI + 8, WID), F32),
        "A": V((6, 9, HEI, WID), F32), "B": V((6, 10, HEI + 8, WID), F32),
        "XSD": V((6, HEI + 8, WID), F32), "XA": V((3, HEI, WID), F32), "XB": V((3, HEI + 8, WID), F32),
        "XF": V((3, HEI, WID), F32), "EX": V((HEI, WID), F32), "XE": V((HEI, WID), F32),
        "X0": V((HEI, WID), F32), "XH": V((HEI, WID), F32),
        "XEs": V((8, WID), F32), "XEr": V((8, WID), F32), "XDr": V((8, WID), F32),
        "XLs": V((48, WID), F32), "XRs": V((48, WID), F32), "XLr": V((48, WID), F32), "XRr": V((48, WID), F32),
        "XWs": V((64, WID), F32), "XWr": V((72, WID), F32), "XCr": V((8, WID), F32),
        "SE": V((3, DEP, HEI, WID), F32), "own": V((6, 8, WID), F32), "red": V((6, big, 8, WID), F32),
        "Wy": V((2, HEI, HEI), BF16), "Wx": V((9, 2, WID, WID), BF16),
        "G": V((DEP, HEI, WID), F32), "Gup": V((DEP, HEI, WID), F32), "Gdn": V((DEP, HEI, WID), F32),
        "HLs": V((2, HEI, WID), F32), "HRs": V((2, HEI, WID), F32),
        "HLr": V((2, HEI, WID), F32), "HRr": V((2, HEI, WID), F32),
        "RU": V((4, HEI, WID), F32), "RD": V((4, HEI, WID), F32), "F": V((DEP, HEI, WID), F32),
    }
    names = list(scratch)

    def kernel(*refs):
        body(sizes, *refs[:6], dict(zip(names, refs[6:])))

    spec = pl.BlockSpec(memory_space=pltpu.VMEM)
    return pl.pallas_call(
        kernel,
        out_shape=(jax.ShapeDtypeStruct(density.shape, F32), jax.ShapeDtypeStruct(load.shape, F32)),
        in_specs=[spec] * 4,
        out_specs=(spec, spec),
        scratch_shapes=[scratch[n] for n in names],
        compiler_params=pltpu.CompilerParams(
            collective_id=0, has_side_effects=True, vmem_limit_bytes=52 * 1024 * 1024),
    )(density, bone, fixed, load)


def solution(mesh):
    sizes = tuple(mesh.shape[name] for name in ("gx", "gy", "gz"))
    placed = (P("gz", "gy", None, "gx"),) * 3 + (P(None, "gz", "gy", None, "gx"),)
    return jax.shard_map(
        functools.partial(on_device, sizes),
        mesh=mesh,
        in_specs=placed,
        out_specs=(P("gz", "gy", None, "gx"), P(None, "gz", "gy", None, "gx")),
        check_vma=False,
    )
```

time: 890 us -> 112 us (0.13)
  blocking collectives: 414 us -> 0 us
  waiting for transfers between devices: 197 us -> 0 us
  other arithmetic: 128 us -> 0 us
  Pallas kernels: 0 us -> 105 us
  starting transfers between devices: 96.2 us -> 0 us
  local copies, waits for them, and re-layouts: 32.1 us -> 6.09 us
  matrix products: 10 us -> 0 us
    psum x4 -> x0, blocking collectives: 399 us -> none  [the longest x2 195 us: inner_sum(): return lax.psum(jnp.sum(values), ('gx', 'gy', 'gz'))]
    ppermute x24 -> x0, waiting for transfers between devices: 197 us -> none  [the longest x6 61.3 us: from_behind(): return lax.ppermute(block, axis, route)]
    pallas_call x0 -> x1, Pallas kernels: none -> 105 us  [on_device(): pl.pallas_call(kernel, out_shape=(jax.ShapeDtypeStruct(density.shape, F32...]
    ppermute x24 -> x0, starting transfers between devices: 92.2 us -> none  [the longest x12 42.1 us: shifted(): lax.ppermute(value, axis, [(source, source + steps) for source in range(i...]
    mul x51 -> x0, other arithmetic: 67.4 us -> none  [the longest x48 65.4 us: lean_forces(): term = moduli * products[component * 8 + node]]
    div x1 -> x0, other arithmetic: 22.1 us -> none  [on_device(): specific = energy / local_density]
    all_to_all x1 -> x0, blocking collectives: 15 us -> none  [to_bricks(): return lax.all_to_all(values, 'gy', split_axis=2, concat_axis=1, tiled=True)]
    slice x16 -> x0, local copies, waits for them, and re-layouts: 13.7 us -> none  [the longest x5 4.05 us: fold_upper(): column = shifted(values[:, :, :, width:], 'gx', 1)]
  transfers between devices with their start and end apart: 25 -> 0, of which waited for: 21 -> 0; matrix products, arithmetic and copies ran while one was open for 1% -> 0% of each run, Pallas kernels for 0% -> 0%
where the time goes in v1:
time: 112 us
  Pallas kernels  105 us (94%)
  local copies, waits for them, and re-layouts  6.09 us (5%)
    pallas_call x1, Pallas kernels, on_device(): pl.pallas_call(kernel, out_shape=(jax.ShapeDtypeStruct(density.shape, F32...  105 us
    unnamed x8, local copies, waits for them, and re-layouts  6.09 us

profile of v1, /device:TPU:1, one launch (start us, length us, event | category | flops | bytes accessed | tf_op | source)
XLA Modules:
  0.0 111.5 jit_solution(3114794641372448132)
XLA Ops:
  0.6 0.0 copy-start
  0.6 1.0 copy-done
  1.6 0.0 copy-start.1
  1.6 1.0 copy-done.1
  2.6 0.0 copy-start.2
  2.6 1.0 copy-done.2
  3.6 104.8 %shard_map.59 = (f32[1,8,96,128]{3,2,1,0:T(8,128)S(1)}, f32[3,1,8,96,128]{4,3,2,1,0:T(8,128)}) custom-call(f32[1,8,96,128]{3,2,1,0:T(8,128)S(1)} %copy-done, s32[1,8,96,128]{3,2,1,0:T(8,128)S(1)} %copy-done.1, s32[1,8,96,128]{3,2,1,0:T(8,128)S(1)} %copy-done.2, f32[3,1,8,96,128]{4,3,2,1,0:T(8,128)} %refs_3_.1), custom_call_target="tpu_custom_call" | custom-call | tf_op jit(solution)/shard_map/pallas_call | solution.py:653
  108.4 0.7 copy.8
  109.2 2.4 %copy.9 = f32[3,1,8,96,128]{4,3,2,1,0:T(8,128)} copy(f32[3,1,8,96,128]{4,3,2,1,0:T(8,128)} %get-tuple-element.5) | data formatting | bytes 2359296
Async XLA Ops:
  0.6 1.0 copy-start
  1.6 1.0 copy-start.1
  2.6 1.0 copy-start.2

commit v2 on v1

v2 whole, which is shorter than its diff:
```python
import functools
import math

import jax
import jax.numpy as jnp
import numpy as np
from jax import lax
from jax.experimental import pallas as pl
from jax.experimental.pallas import tpu as pltpu
from jax.sharding import PartitionSpec as P

MESH = pl.DeviceIdType.MESH
RAD = 24
MARROW = 0.1
REMODEL = 0.25
FLOOR = 0.2
CEILING = 1.0
EPSILON = 1e-06
DEP = 8
HEI = 96
WID = 128
F32 = jnp.float32
BF16 = jnp.bfloat16


def element_stiffness():
    poisson = 0.3
    lame = poisson / ((1.0 + poisson) * (1.0 - 2.0 * poisson))
    shear = 0.5 / (1.0 + poisson)
    elastic = np.zeros((6, 6))
    elastic[:3, :3] = lame
    for index in range(3):
        elastic[index, index] += 2.0 * shear
        elastic[index + 3, index + 3] = shear
    points = [0.5 - 0.5 / math.sqrt(3.0), 0.5 + 0.5 / math.sqrt(3.0)]
    matrix = np.zeros((24, 24))
    for point_z in points:
        for point_y in points:
            for point_x in points:
                strain = np.zeros((6, 24))
                for corner_z in range(2):
                    for corner_y in range(2):
                        for corner_x in range(2):
                            node = 4 * corner_z + 2 * corner_y + corner_x
                            shape_x = point_x if corner_x else 1.0 - point_x
                            shape_y = point_y if corner_y else 1.0 - point_y
                            shape_z = point_z if corner_z else 1.0 - point_z
                            slope_x = 1.0 if corner_x else -1.0
                            slope_y = 1.0 if corner_y else -1.0
                            slope_z = 1.0 if corner_z else -1.0
                            along_x = slope_x * shape_y * shape_z
                            along_y = shape_x * slope_y * shape_z
                            along_z = shape_x * shape_y * slope_z
                            strain[0, node] = along_x
                            strain[1, 8 + node] = along_y
                            strain[2, 16 + node] = along_z
                            strain[3, node] = along_y
                            strain[3, 8 + node] = along_x
                            strain[4, 8 + node] = along_z
                            strain[4, 16 + node] = along_y
                            strain[5, node] = along_z
                            strain[5, 16 + node] = along_x
                matrix = matrix + strain.T @ elastic @ strain / 8.0
    return matrix


KE = element_stiffness()
HAAR1 = np.array([[1.0, 1.0], [-1.0, 1.0]])
HAAR = np.kron(np.eye(3), np.kron(HAAR1, np.kron(HAAR1, HAAR1)))
KH = HAAR @ KE @ HAAR.T / 64.0
DIAG = float(KE[0, 0])
GROUPS = ((1, 10, 20), (2, 9), (4, 17), (12, 18), (3, 22), (5, 14), (11, 21), (6, 13, 19), (7,), (15,), (23,))
LAMBDA = math.exp(-1.0 / 12.0)
NORMAL = 1.0 / (1.0 + 2.0 * sum(LAMBDA**d for d in range(1, RAD + 1)))


def stress(m):
    out = [None] * 24
    for group in GROUPS:
        first = group[0]
        diag = float(KH[first, first])
        if len(group) == 1:
            out[first] = diag * m[first]
            continue
        off = float(KH[first, group[1]])
        total = m[first]
        for k in group[1:]:
            total = total + m[k]
        common = off * total
        for k in group:
            out[k] = common if abs(diag - off) < 1e-12 else common + (diag - off) * m[k]
    return out


def bilinear(m, f):
    total = None
    for k in range(24):
        if f[k] is not None:
            total = m[k] * f[k] if total is None else total + m[k] * f[k]
    return total


def zmodes(lo, hi):
    m = [None] * 24
    for c in range(3):
        for p in range(4):
            m[c * 8 + p] = hi[c * 4 + p] + lo[c * 4 + p]
            m[c * 8 + 4 + p] = hi[c * 4 + p] - lo[c * 4 + p]
    return m


def minus(a, b):
    return -b if a is None else a - b


def plus(a, b):
    return b if a is None else a + b


def split(value):
    hi = value.astype(BF16)
    return hi, (value - hi.astype(F32)).astype(BF16)


def dot(a, b):
    return jnp.dot(a, b, preferred_element_type=F32)


def tap(distance):
    return jnp.where(distance <= RAD, NORMAL * jnp.exp(distance.astype(F32) * (-1.0 / 12.0)), 0.0)


def power(exponent):
    return jnp.exp(exponent.astype(F32) * (-1.0 / 12.0))


def kept(index, size):
    ends = power(jnp.minimum(index, RAD) + 1) + power(jnp.minimum(size - 1 - index, RAD) + 1)
    return NORMAL * (1.0 + (2.0 * LAMBDA - ends) * (1.0 / (1.0 - LAMBDA)))


def fold(value):
    return jnp.sum(value.reshape(HEI // 8, 8, WID), axis=0)


def rows(value):
    return jnp.sum(value, axis=0, keepdims=True)


def body(sizes, dens_h, bone_h, fixed_h, load_h, out_d, out_u, s):
    GX, GY, GZ = sizes
    S = GY * GZ
    gx, gy, gz = lax.axis_index("gx"), lax.axis_index("gy"), lax.axis_index("gz")
    slab = gz * GY + gy
    lane = lax.broadcasted_iota(jnp.int32, (HEI, WID), 1)
    rowi = lax.broadcasted_iota(jnp.int32, (HEI, WID), 0)

    def device(dx=0, ds=0):
        t = lax.rem(slab + ds + S, S)
        return (lax.rem(gx + dx + GX, GX), lax.rem(t, GY), lax.div(t, GY))

    def flag(cond):
        return jnp.where(cond, 1.0, 0.0).astype(F32)

    has_left, has_right = flag(gx > 0), flag(gx < GX - 1)
    has_down, has_up = flag(slab > 0), flag(slab < S - 1)

    count = [0]
    sends = []

    def remote(src, dst, target):
        k = count[0]
        count[0] += 1
        copy = pltpu.make_async_remote_copy(
            src_ref=src, dst_ref=dst, send_sem=s["send"].at[k], recv_sem=s["recv"].at[k],
            device_id=target, device_id_type=MESH)
        copy.start()
        sends.append(copy)
        return copy

    dens, bone, fixed, load = s["dens"], s["bone"], s["fixed"], s["load"]
    loads = []
    for k, (src, dst) in enumerate(((dens_h, dens), (bone_h, bone), (fixed_h, fixed), (load_h, load))):
        copy = pltpu.make_async_copy(src, dst, s["local"].at[k])
        copy.start()
        loads.append(copy)

    barrier = pltpu.get_barrier_semaphore()
    peers = [device(-1), device(1), device(0, 1), device(0, -1), device(1, 1), device(-1, -1),
             device(0, 3), device(0, -3)]
    for k in range(2, GX - 1):
        peers.append((lax.rem(gx + k, GX), gy, gz))
    for k in range(1, GY):
        peers.append((gx, lax.rem(gy + k, GY), gz))
    for k in range(1, GZ):
        peers.append((gx, gy, lax.rem(gz + k, GZ)))
    for peer in peers:
        pl.semaphore_signal(barrier, inc=1, device_id=peer, device_id_type=MESH)

    zero8 = jnp.zeros((8, WID), F32)

    @pl.loop(0, 10)
    def _(zz):
        for k in range(6):
            s["SDs"][k, zz, pl.ds(HEI, 8)] = zero8
            s["SDw"][k, zz, pl.ds(HEI, 8)] = zero8
            s["B"][k, zz, pl.ds(0, 8)] = zero8

    for k in range(6):
        s["XSD"][k, pl.ds(HEI, 8)] = zero8
    for k in range(3):
        s["XB"][k, pl.ds(0, 8)] = zero8

    E, R = s["E"], s["R"]
    loads[0].wait()
    loads[1].wait()

    @pl.loop(0, DEP)
    def _(z):
        b = bone[0, z].astype(F32)
        d = dens[0, z]
        E[z + 1] = b * d * d + (1.0 - b) * MARROW

    def pack(get, slots, src):
        acc = jnp.zeros((HEI, WID), F32)
        for index, k in slots:
            acc = jnp.where(lane == k, pltpu.roll(get(index), (k - src) % WID, 1), acc)
        return acc

    def turned(acc):
        full = jnp.concatenate([acc, jnp.zeros((WID - HEI, WID), F32)], axis=0)
        return jnp.transpose(full)

    def unturned(ref, number):
        got = ref[...]
        full = jnp.concatenate([got, jnp.zeros((WID - number, WID), F32)], axis=0)
        return jnp.transpose(full)[:HEI]

    s["XEs"][...] = turned(pack(lambda z: E[z + 1], [(z, z) for z in range(DEP)], WID - 1))[:8]
    loads[2].wait()
    loads[3].wait()

    @pl.loop(0, DEP)
    def _(z):
        f = 1.0 - fixed[0, z].astype(F32)
        for c in range(3):
            R[c, z] = f * load[c, 0, z]

    pl.semaphore_wait(barrier, len(peers))
    c_xe = remote(s["XEs"], s["XEr"], device(1))
    c_e = remote(E.at[DEP], E.at[0], device(0, 1))
    c_r = remote(R.at[:, 0], s["R8"], device(0, -1))
    c_xd = remote(s["XEs"], s["XDr"], device(1, 1))

    T = s["T"]
    s0, Q = s["s0"], s["Q"]

    def inplane(e, edge):
        ex = e + jnp.where(lane == 0, edge, pltpu.roll(e, 1, 1))
        return ex + jnp.where(rowi == 0, 0.0, pltpu.roll(ex, 1, 0))

    def flat(z):
        T[z + 1] = inplane(E[z + 1], pltpu.roll(s["XE"][...], lax.rem(WID - z, WID), 1))

    def start(z):
        inv = 1.0 / (DIAG * (T[z] + T[z + 1]))
        Q[z] = (1.0 - fixed[0, z].astype(F32)) * inv
        for c in range(3):
            s0[c, z + 1] = R[c, z] * inv

    c_xe.wait_recv()
    s["XE"][...] = unturned(s["XEr"], 8) * has_left
    flat(DEP - 1)
    flat(DEP - 2)
    start(DEP - 1)
    c_s = remote(s0.at[:, DEP], s0.at[:, 0], device(0, 1))
    flat(0)
    c_t = remote(T.at[1], T.at[DEP + 1], device(0, -1))
    pl.loop(1, DEP - 2)(flat)
    pl.loop(1, DEP - 1)(start)

    def columns(planes, name):
        slots = [((c, zz), 16 * c + zz) for c in range(3) for zz in planes]
        first = pack(lambda i: s0[i[0], i[1]], slots, 0)
        last = pack(lambda i: s0[i[0], i[1]], slots, WID - 1)
        s["XLs" + name][...] = turned(first)[:48]
        s["XRs" + name][...] = turned(last)[:48]
        return first, (remote(s["XLs" + name], s["XRr" + name], device(-1)),
                       remote(s["XRs" + name], s["XLr" + name], device(1)))

    first, pair = columns(range(2, 9), "1")
    s["X0"][...] = first

    far_y = jnp.abs(lax.broadcasted_iota(jnp.int32, (HEI, HEI), 0) - lax.broadcasted_iota(jnp.int32, (HEI, HEI), 1))
    s["Wy"][0], s["Wy"][1] = split(tap(far_y))
    row = lax.broadcasted_iota(jnp.int32, (WID, WID), 0)
    col = lax.broadcasted_iota(jnp.int32, (WID, WID), 1)
    s["Wx"][0, 0], s["Wx"][0, 1] = split(tap(jnp.abs(row - col)))
    for j in range(4):
        inside = (row >= 32 * j) & (row < 32 * j + 32)
        right = jnp.where(inside, tap(jnp.abs(WID + row - 32 * j - col)), 0.0)
        left = jnp.where(inside, tap(jnp.abs(col + 32 - row + 32 * j)), 0.0)
        s["Wx"][1 + j, 0], s["Wx"][1 + j, 1] = split(left)
        s["Wx"][5 + j, 0], s["Wx"][5 + j, 1] = split(right)
    s["W2"][...] = kept(gx * WID + lane, GX * WID) * kept(rowi, HEI)

    def edges(got):
        for c in range(3):
            s["XSD"][2 * c, pl.ds(0, HEI)] = pltpu.roll(s["X0"][...] + got, (WID - 16 * c) % WID, 1)
            s["XSD"][2 * c + 1, pl.ds(0, HEI)] = pltpu.roll(s["X0"][...] - got, (WID - 16 * c) % WID, 1)

    def arrive(pair, name):
        for copy in pair:
            copy.wait_recv()
        s["XH"][...] = unturned(s["XRr" + name], 48) * has_right
        return unturned(s["XLr" + name], 48)

    def xstage(field, SD, shift, zz):
        for c in range(3):
            v = field[c, zz]
            h = pltpu.roll(s["XH"][...], shift(c, zz), 1)
            v1 = jnp.where(lane == WID - 1, h, pltpu.roll(v, WID - 1, 1))
            SD[2 * c, zz, pl.ds(0, HEI)] = v1 + v
            SD[2 * c + 1, zz, pl.ds(0, HEI)] = v1 - v

    def place_s(c, zz):
        return WID - 1 - 16 * c - zz

    def place_w(c, z):
        return WID - 1 - 8 * z - c

    def planar(SD, zz, y0):
        out = []
        for c in range(3):
            a0, a1 = SD[2 * c, zz, pl.ds(y0, 8)], SD[2 * c, zz, pl.ds(y0 + 1, 8)]
            b0, b1 = SD[2 * c + 1, zz, pl.ds(y0, 8)], SD[2 * c + 1, zz, pl.ds(y0 + 1, 8)]
            out += [a1 + a0, b1 + b0, a1 - a0, b1 - b0]
        return out

    A, B = s["A"], s["B"]

    def element(lo, hi, zz, y0):
        f = stress(zmodes(lo, hi))
        e = E[zz, pl.ds(y0, 8)]
        f = [None if v is None else v * e for v in f]
        up = [plus(f[c * 8 + p], f[c * 8 + 4 + p]) for c in range(3) for p in range(4)]
        down = [minus(f[c * 8 + p], f[c * 8 + 4 + p]) for c in range(3) for p in range(4)]
        return down, up

    def put(g, zz, y0, more=False):
        for c in range(3):
            for ix in range(2):
                a = g[4 * c + ix] - g[4 * c + 2 + ix]
                b = g[4 * c + ix] + g[4 * c + 2 + ix]
                if more:
                    a = a + A[2 * c + ix, zz, pl.ds(y0, 8)]
                    b = b + B[2 * c + ix, zz, pl.ds(y0 + 8, 8)]
                A[2 * c + ix, zz, pl.ds(y0, 8)] = a
                B[2 * c + ix, zz, pl.ds(y0 + 8, 8)] = b

    def both(g, h):
        return [u + v for u, v in zip(g, h)]

    def edge_elements(y0):
        lo = []
        for c in range(3):
            a0, a1 = s["XSD"][2 * c, pl.ds(y0, 8)], s["XSD"][2 * c, pl.ds(y0 + 1, 8)]
            b0, b1 = s["XSD"][2 * c + 1, pl.ds(y0, 8)], s["XSD"][2 * c + 1, pl.ds(y0 + 1, 8)]
            lo += [a1 + a0, b1 + b0, a1 - a0, b1 - b0]
        hi = [pltpu.roll(v, WID - 1, 1) for v in lo]
        f = stress(zmodes(lo, hi))
        e = s["EX"][pl.ds(y0, 8)]
        f = [None if v is None else v * e for v in f]
        for c in range(3):
            g = []
            for p in range(4):
                up = plus(f[c * 8 + p], f[c * 8 + 4 + p])
                down = minus(f[c * 8 + p], f[c * 8 + 4 + p])
                g.append(down + pltpu.roll(up, 1, 1))
            s["XA"][c, pl.ds(y0, 8)] = (g[0] - g[2]) + (g[1] - g[3])
            s["XB"][c, pl.ds(y0 + 8, 8)] = (g[0] + g[2]) + (g[1] + g[3])

    def chunks(step):
        @pl.loop(0, HEI // 8)
        def _(i):
            step(pl.multiple_of(i * 8, 8))

    w0 = s["w0"]

    def image(z, sums):
        gamma, delta, eps = sums
        q = Q[z]
        for c in range(3):
            gs = A[2 * c, z + 1] + B[2 * c, z + 1, pl.ds(7, HEI)]
            gd = A[2 * c + 1, z + 1] + B[2 * c + 1, z + 1, pl.ds(7, HEI)]
            edge = pltpu.roll(s["XA"][c] + s["XB"][c, pl.ds(7, HEI)], WID - 1 - z, 1)
            im = (gs - gd) + jnp.where(lane == 0, edge, pltpu.roll(gs + gd, 1, 1))
            w = im * q
            w0[c, z] = w
            v = s0[c, z + 1]
            gamma = gamma + fold(R[c, z] * v)
            delta = delta + fold(v * im)
            eps = eps + fold(w * im)
        return gamma, delta, eps

    s["EX"][...] = pltpu.roll(s["XE"][...], 1, 1)
    s["XL1"][...] = arrive(pair, "1")
    edges(s["XL1"][...])
    pl.loop(2, 9)(lambda zz: xstage(s0, s["SDs"], place_s, zz))

    def early(y0):
        def plane(zz, carry):
            lo, above = carry
            hi = planar(s["SDs"], zz + 1, y0)
            down, up = element(lo, hi, zz, y0)
            put(both(above, down), zz, y0)
            return tuple(hi), tuple(up)

        top = lax.fori_loop(2, DEP, plane, (tuple(planar(s["SDs"], 2, y0)), (zero8,) * 12))[1]
        put(top, DEP, y0)
        edge_elements(y0)

    chunks(early)
    sums = lax.fori_loop(2, DEP - 1, image, (zero8, zero8, zero8))

    c_xd.wait_recv()
    c_e.wait_recv()
    E[0] = E[0] * has_down
    corner = pltpu.roll(unturned(s["XDr"], 8) * (has_left * has_down), WID - 7, 1)
    T[0] = inplane(E[0], corner)
    start(0)
    s["EX"][...] = jnp.where(lane == 0, corner, s["EX"][...])
    c_r.wait_recv()
    c_t.wait_recv()
    inv8 = has_up / (DIAG * (T[DEP] + has_up * T[DEP + 1]))
    for c in range(3):
        s0[c, DEP + 1] = s["R8"][c] * inv8
    c_s.wait_recv()

    first, pair = columns((0, 1, 9), "2")
    s["X0"][...] = s["X0"][...] + first
    edges(s["XL1"][...] + arrive(pair, "2"))
    for zz in (0, 1, 9):
        xstage(s0, s["SDs"], place_s, zz)

    def late(y0):
        SD = s["SDs"]
        n0, n1, n2 = planar(SD, 0, y0), planar(SD, 1, y0), planar(SD, 2, y0)
        up = element(n0, n1, 0, y0)[1]
        down, above = element(n1, n2, 1, y0)
        put(both(up, down), 1, y0)
        put(above, 2, y0, more=True)
        put(element(planar(SD, 8, y0), planar(SD, 9, y0), DEP, y0)[0], DEP, y0, more=True)
        edge_elements(y0)

    chunks(late)
    sums = image(0, sums)
    c_w = remote(w0.at[:, 0], w0.at[:, DEP], device(0, -1))
    sums = image(1, sums)
    gamma, delta, eps = image(DEP - 1, sums)

    slots = [((c, z), 8 * z + c) for z in range(DEP) for c in range(3)]
    s["XWs"][...] = turned(pack(lambda i: w0[i[0], i[1]], slots, 0))[:64]
    c_xw = remote(s["XWs"], s["XWr"].at[pl.ds(0, 64)], device(-1))
    c_xc = remote(s["XWs"].at[pl.ds(0, 8)], s["XCr"], device(-1, -1))

    SDs, SDw, SE = s["SDs"], s["SDw"], s["SE"]

    def self_energy(y0):
        def plane(z, lo):
            hi = planar(SDs, z + 2, y0)
            m = zmodes(lo, hi)
            SE[0, z, pl.ds(y0, 8)] = bilinear(m, stress(m))
            return tuple(hi)
        lax.fori_loop(0, DEP, plane, tuple(planar(SDs, 1, y0)))

    def w_energy(low, high):
        def step(y0):
            def plane(z, lo):
                hi = planar(SDw, z + 1, y0)
                m = zmodes(lo, hi)
                SE[2, z, pl.ds(y0, 8)] = bilinear(m, stress(m))
                return tuple(hi)
            lax.fori_loop(low, high, plane, tuple(planar(SDw, low, y0)))
        return step

    def cross_energy(low, high):
        def step(y0):
            def plane(z, carry):
                los, lows = carry
                his, hiw = planar(SDs, z + 2, y0), planar(SDw, z + 1, y0)
                SE[1, z, pl.ds(y0, 8)] = bilinear(zmodes(lows, hiw), stress(zmodes(los, his)))
                return tuple(his), tuple(hiw)
            lax.fori_loop(low, high, plane, (tuple(planar(SDs, low + 1, y0)), tuple(planar(SDw, low, y0))))
        return step

    def per_density(z, sums):
        zeta, m0, m1, m2 = sums
        e = E[z + 1]
        g = 0.5 * e / dens[0, z]
        weight = s["W2"][...] * kept(jnp.full((HEI, WID), slab * DEP + z, jnp.int32), S * DEP)
        zeta = zeta + fold(SE[2, z] * e)
        out = []
        for i, m in enumerate((m0, m1, m2)):
            v = SE[i, z] * g
            SE[i, z] = v
            out.append(m + fold(v * weight))
        return (zeta, *out)

    HLs, HRs, HLr, HRr = s["HLs"], s["HRs"], s["HLr"], s["HRr"]

    def send_sides(b):
        @pl.loop(0, 3)
        def _(i):
            acc_l = acc_r = None
            for j in range(4):
                v = SE[i, 4 * b + j]
                mine = (lane >= 32 * j) & (lane < 32 * j + 32)
                to_l = pltpu.roll(v, 32 * j, 1) if j else v
                to_r = pltpu.roll(v, (32 * j - 96) % WID, 1) if (32 * j - 96) % WID else v
                acc_l = to_l if acc_l is None else jnp.where(mine, to_l, acc_l)
                acc_r = to_r if acc_r is None else jnp.where(mine, to_r, acc_r)
            HLs[b, i] = acc_l
            HRs[b, i] = acc_r
        return remote(HLs.at[b], HRr.at[b], device(-1)), remote(HRs.at[b], HLr.at[b], device(1))

    chunks(self_energy)
    c_xw.wait_recv()
    s["XH"][...] = unturned(s["XWr"], 72) * has_right
    pl.loop(0, DEP)(lambda z: xstage(w0, SDw, place_w, z))
    chunks(w_energy(0, DEP - 1))
    chunks(cross_energy(0, DEP - 1))
    forms = lax.fori_loop(0, DEP - 1, per_density, (zero8,) * 4)
    sides = [send_sides(0)]

    c_xc.wait_recv()
    c_w.wait_recv()
    s["XWr"][pl.ds(64, 8)] = s["XCr"][...] * has_up
    s["XH"][...] = unturned(s["XWr"], 72) * has_right
    for c in range(3):
        w0[c, DEP] = w0[c, DEP] * has_up
    xstage(w0, SDw, place_w, DEP)
    chunks(w_energy(DEP - 1, DEP))
    chunks(cross_energy(DEP - 1, DEP))
    forms = per_density(DEP - 1, forms)

    axes = ((GX, gx, lambda p: (p, gy, gz)), (GY, gy, lambda p: (gx, p, gz)), (GZ, gz, lambda p: (gx, gy, p)))
    own, red = s["own"], s["red"]

    def reduce_start(stage):
        n, me, target = axes[stage]
        return [remote(own.at[stage], red.at[stage, me], target(lax.rem(me + k, n))) for k in range(1, n)]

    def reduce_end(stage, copies):
        n, me, _ = axes[stage]
        for copy in copies:
            copy.wait_recv()
        red[stage, me] = own[stage]
        total = red[stage, 0]
        for k in range(1, n):
            total = total + red[stage, k]
        return total

    own[0] = jnp.concatenate([rows(v) for v in (gamma, delta, eps, *forms)] + [jnp.zeros((1, WID), F32)], axis=0)
    copies = reduce_start(0)
    sides.append(send_sides(1))

    def smooth_y(v):
        hi, lo = split(v)
        return dot(s["Wy"][0], hi) + dot(s["Wy"][1], hi) + dot(s["Wy"][0], lo)

    def smooth_x(v, k):
        hi, lo = split(v)
        return dot(hi, s["Wx"][k, 0]) + dot(hi, s["Wx"][k, 1]) + dot(lo, s["Wx"][k, 0])

    @pl.loop(0, DEP)
    def _(z):
        for i in range(3):
            SE[i, z] = smooth_y(SE[i, z])

    own[1] = reduce_end(0, copies)
    copies = reduce_start(1)

    for pair in sides:
        for copy in pair:
            copy.wait_recv()
    for b in range(2):
        @pl.loop(0, 3)
        def _(i, b=b):
            HLr[b, i] = smooth_y(HLr[b, i] * has_left)
            HRr[b, i] = smooth_y(HRr[b, i] * has_right)

    own[2] = reduce_end(1, copies)
    copies = reduce_start(2)

    for b in range(2):
        @pl.loop(0, 4)
        def _(j, b=b):
            for i in range(3):
                SE[i, 4 * b + j] = (smooth_x(SE[i, 4 * b + j], 0) + smooth_x(HLr[b, i], 1 + j)
                                    + smooth_x(HRr[b, i], 5 + j))

    total = jnp.sum(reduce_end(2, copies), axis=1, keepdims=True)
    g0, d0, ep, ze = total[0:1], total[1:2], total[2:3], total[3:4]
    alpha = g0 / d0
    g1 = g0 - 2.0 * alpha * d0 + alpha * alpha * ep
    beta = g1 / g0
    d1 = (1.0 + beta) * (1.0 + beta) * d0 - 2.0 * alpha * (1.0 + beta) * ep + alpha * alpha * ze
    alpha1 = g1 / d1
    a1 = alpha + alpha1 * (1.0 + beta)
    b1 = -(alpha1 * alpha)
    ca = jnp.broadcast_to(a1, (HEI, WID))
    cb = jnp.broadcast_to(b1, (HEI, WID))
    caa, cab, cbb = a1 * a1, 2.0 * (a1 * b1), b1 * b1
    mean = (caa * total[4:5] + cab * total[5:6] + cbb * total[6:7]) / float(S * DEP * HEI * WID * GX)
    scale = NORMAL * jnp.broadcast_to(1.0 / (mean + EPSILON), (HEI, WID))
    caa, cab, cbb = (jnp.broadcast_to(v, (HEI, WID)) for v in (caa, cab, cbb))

    G, Gup, Gdn, F = s["G"], s["Gup"], s["Gdn"], s["F"]

    @pl.loop(0, DEP)
    def _(z):
        G[z] = caa * SE[0, z] + cab * SE[1, z] + cbb * SE[2, z]

    low = G[DEP - 1]
    high = G[0]
    for k in range(1, DEP):
        low = LAMBDA * low + G[DEP - 1 - k]
        high = LAMBDA * high + G[k]
    RU, RD = s["RU"], s["RD"]
    RU[0] = low
    RD[0] = high
    c_u0 = remote(RU.at[0], RU.at[1], device(0, -1))
    c_d0 = remote(RD.at[0], RD.at[1], device(0, 1))

    def planes(k):
        z = DEP - 1 - k
        return remote(G.at[k], Gup.at[k], device(0, -3)), remote(G.at[z], Gdn.at[z], device(0, 3))

    far = [planes(k) for k in range(4)]

    acc = None
    for z in range(DEP):
        acc = G[z] if z == 0 else LAMBDA * acc + G[z]
        F[z] = acc
    acc = jnp.zeros((HEI, WID), F32)
    for z in range(DEP - 2, -1, -1):
        acc = LAMBDA * (acc + G[z + 1])
        F[z] = F[z] + acc

    at1, at3 = flag(slab + 1 < S), flag(slab + 3 < S)
    bt1, bt3 = flag(slab >= 1), flag(slab >= 3)
    c_u0.wait_recv()
    c_d0.wait_recv()
    RU[2] = RU[0] + (LAMBDA**DEP * at1) * RU[1]
    RD[2] = RD[0] + (LAMBDA**DEP * bt1) * RD[1]
    c_u1 = remote(RU.at[2], RU.at[3], device(0, -1))
    c_d1 = remote(RD.at[2], RD.at[3], device(0, 1))
    far += [planes(k) for k in range(4, DEP)]

    @pl.loop(0, DEP)
    def _(z):
        for c in range(3):
            s["U"][c, 0, z] = ca * s0[c, z + 1] + cb * w0[c, z]

    stores = [pltpu.make_async_copy(s["U"], out_u, s["local"].at[4])]
    stores[0].start()

    c_u1.wait_recv()
    c_d1.wait_recv()
    near_u, near_d = at1 * RU[3], bt1 * RD[3]
    for z in range(DEP):
        F[z] = F[z] + LAMBDA ** (DEP - z) * near_u + LAMBDA ** (z + 1) * near_d

    up_scale, dn_scale = at3 * LAMBDA**RAD, bt3 * LAMBDA**RAD
    RR = s["RR"]

    def finish_plane(z, value):
        b = bone[0, z].astype(F32)
        new = dens[0, z] + REMODEL * b * (value * scale - 1.0)
        s["D"][0, z] = jnp.clip(new, FLOOR, CEILING)
        copy = pltpu.make_async_copy(s["D"].at[0, z], out_d.at[0, z], s["local"].at[5 + z])
        copy.start()
        stores.append(copy)

    for k in range(DEP):
        z = DEP - 1 - k
        far[k][0].wait_recv()
        far[k][1].wait_recv()
        up = up_scale * Gup[k]
        down = dn_scale * Gdn[z]
        if k:
            up = up + (1.0 / LAMBDA) * RR[0]
            down = down + (1.0 / LAMBDA) * RR[1]
        RR[0] = up
        RR[1] = down
        if k < DEP // 2:
            F[k] = F[k] + up
            F[z] = F[z] + down
        else:
            finish_plane(k, F[k] + up)
            finish_plane(z, F[z] + down)

    for copy in stores:
        copy.wait()
    for copy in sends:
        copy.wait_send()


def on_device(sizes, density, bone, fixed, load):
    GX, GY, GZ = sizes
    copies = 4 + 2 + 4 + 3 + 4 + (GX + GY + GZ - 3) + 4 + 16
    V = pltpu.VMEM
    plane, tall, thin = (HEI, WID), (HEI + 8, WID), (48, WID)
    scratch = {
        "send": pltpu.SemaphoreType.DMA((copies,)),
        "recv": pltpu.SemaphoreType.DMA((copies,)),
        "local": pltpu.SemaphoreType.DMA((13,)),
        "U": V(load.shape, F32), "D": V(density.shape, F32),
        "dens": V(density.shape, F32), "bone": V(bone.shape, jnp.int32), "fixed": V(fixed.shape, jnp.int32),
        "load": V(load.shape, F32),
        "E": V((9, *plane), F32), "R": V((3, DEP, *plane), F32), "R8": V((3, *plane), F32),
        "T": V((10, *plane), F32), "Q": V((DEP, *plane), F32),
        "s0": V((3, 10, *plane), F32), "w0": V((3, 9, *plane), F32),
        "SDs": V((6, 10, *tall), F32), "SDw": V((6, 10, *tall), F32),
        "A": V((6, 9, *plane), F32), "B": V((6, 10, *tall), F32),
        "XSD": V((6, *tall), F32), "XA": V((3, *plane), F32), "XB": V((3, *tall), F32),
        "EX": V(plane, F32), "XE": V(plane, F32), "X0": V(plane, F32), "XH": V(plane, F32), "XL1": V(plane, F32),
        "XEs": V((8, WID), F32), "XEr": V((8, WID), F32), "XDr": V((8, WID), F32),
        "XLs1": V(thin, F32), "XRs1": V(thin, F32), "XLr1": V(thin, F32), "XRr1": V(thin, F32),
        "XLs2": V(thin, F32), "XRs2": V(thin, F32), "XLr2": V(thin, F32), "XRr2": V(thin, F32),
        "XWs": V((64, WID), F32), "XWr": V((72, WID), F32), "XCr": V((8, WID), F32),
        "SE": V((3, DEP, *plane), F32), "own": V((3, 8, WID), F32), "red": V((3, max(sizes), 8, WID), F32),
        "Wy": V((2, HEI, HEI), BF16), "Wx": V((9, 2, WID, WID), BF16), "W2": V(plane, F32),
        "G": V((DEP, *plane), F32), "Gup": V((DEP, *plane), F32), "Gdn": V((DEP, *plane), F32),
        "HLs": V((2, 3, *plane), F32), "HRs": V((2, 3, *plane), F32),
        "HLr": V((2, 3, *plane), F32), "HRr": V((2, 3, *plane), F32),
        "RU": V((4, *plane), F32), "RD": V((4, *plane), F32), "F": V((DEP, *plane), F32), "RR": V((2, *plane), F32),
    }
    names = list(scratch)

    def kernel(*refs):
        body(sizes, *refs[:6], dict(zip(names, refs[6:])))

    outer = pl.BlockSpec(memory_space=pltpu.HBM)
    return pl.pallas_call(
        kernel,
        out_shape=(jax.ShapeDtypeStruct(density.shape, F32), jax.ShapeDtypeStruct(load.shape, F32)),
        in_specs=[outer] * 4,
        out_specs=(outer, outer),
        scratch_shapes=[scratch[n] for n in names],
        compiler_params=pltpu.CompilerParams(
            collective_id=0, has_side_effects=True, vmem_limit_bytes=56 * 1024 * 1024),
    )(density, bone, fixed, load)


def solution(mesh):
    sizes = tuple(mesh.shape[name] for name in ("gx", "gy", "gz"))
    placed = (P("gz", "gy", None, "gx"),) * 3 + (P(None, "gz", "gy", None, "gx"),)
    return jax.shard_map(
        functools.partial(on_device, sizes),
        mesh=mesh,
        in_specs=placed,
        out_specs=(P("gz", "gy", None, "gx"), P(None, "gz", "gy", None, "gx")),
        check_vma=False,
    )
```

time: 112 us -> 95.8 us (0.86)
  the two profiles are of different devices: /device:TPU:1 before, /device:TPU:6 now
where the time goes in v2:
time: 95.8 us; the launch traced here: 95.6 us
  Pallas kernels  90.8 us (95%)
  local copies, waits for them, and re-layouts  4.13 us (4%)
    pallas_call x1, Pallas kernels, on_device(): pl.pallas_call(kernel, out_shape=(jax.ShapeDtypeStruct(density.shape, F32...  90.8 us
    unnamed x2, local copies, waits for them, and re-layouts  4.13 us

profile of v2, /device:TPU:6, one launch (start us, length us, event | category | flops | bytes accessed | tf_op | source)
XLA Modules:
  0.0 95.6 jit_solution(10950872718515507023)
XLA Ops:
  0.6 90.8 %shard_map.59 = (f32[1,8,96,128]{3,2,1,0:T(8,128)}, f32[3,1,8,96,128]{4,3,2,1,0:T(8,128)}) custom-call(f32[1,8,96,128]{3,2,1,0:T(8,128)} %refs_0_.1, s32[1,8,96,128]{3,2,1,0:T(8,128)} %refs_1_.1, s32[1,8,96,128]{3,2,1,0:T(8,128)} %refs_2_.1, f32[3,1,8,96,128]{4,3,2,1,0:T(8,128)} %refs_3_.1), custom_call_target="tpu_custom_call" | custom-call | tf_op jit(solution)/shard_map/pallas_call | solution.py:746
  91.5 1.8 %copy.8 = f32[1,8,96,128]{3,2,1,0:T(8,128)} copy(f32[1,8,96,128]{3,2,1,0:T(8,128)} %get-tuple-element.4) | data formatting | bytes 786432
  93.2 2.4 %copy.9 = f32[3,1,8,96,128]{4,3,2,1,0:T(8,128)} copy(f32[3,1,8,96,128]{4,3,2,1,0:T(8,128)} %get-tuple-element.5) | data formatting | bytes 2359296

commit v3 on v2

--- a/solution.py
+++ b/solution.py
@@ -187,7 +187,7 @@
 
     barrier = pltpu.get_barrier_semaphore()
     peers = [device(-1), device(1), device(0, 1), device(0, -1), device(1, 1), device(-1, -1),
-             device(0, 3), device(0, -3)]
+             device(0, 3), device(0, -3), device(0, 2), device(0, -2)]
     for k in range(2, GX - 1):
         peers.append((lax.rem(gx + k, GX), gy, gz))
     for k in range(1, GY):
@@ -210,86 +210,6 @@
         s["XSD"][k, pl.ds(HEI, 8)] = zero8
     for k in range(3):
         s["XB"][k, pl.ds(0, 8)] = zero8
-
-    E, R = s["E"], s["R"]
-    loads[0].wait()
-    loads[1].wait()
-
-    @pl.loop(0, DEP)
-    def _(z):
-        b = bone[0, z].astype(F32)
-        d = dens[0, z]
-        E[z + 1] = b * d * d + (1.0 - b) * MARROW
-
-    def pack(get, slots, src):
-        acc = jnp.zeros((HEI, WID), F32)
-        for index, k in slots:
-            acc = jnp.where(lane == k, pltpu.roll(get(index), (k - src) % WID, 1), acc)
-        return acc
-
-    def turned(acc):
-        full = jnp.concatenate([acc, jnp.zeros((WID - HEI, WID), F32)], axis=0)
-        return jnp.transpose(full)
-
-    def unturned(ref, number):
-        got = ref[...]
-        full = jnp.concatenate([got, jnp.zeros((WID - number, WID), F32)], axis=0)
-        return jnp.transpose(full)[:HEI]
-
-    s["XEs"][...] = turned(pack(lambda z: E[z + 1], [(z, z) for z in range(DEP)], WID - 1))[:8]
-    loads[2].wait()
-    loads[3].wait()
-
-    @pl.loop(0, DEP)
-    def _(z):
-        f = 1.0 - fixed[0, z].astype(F32)
-        for c in range(3):
-            R[c, z] = f * load[c, 0, z]
-
-    pl.semaphore_wait(barrier, len(peers))
-    c_xe = remote(s["XEs"], s["XEr"], device(1))
-    c_e = remote(E.at[DEP], E.at[0], device(0, 1))
-    c_r = remote(R.at[:, 0], s["R8"], device(0, -1))
-    c_xd = remote(s["XEs"], s["XDr"], device(1, 1))
-
-    T = s["T"]
-    s0, Q = s["s0"], s["Q"]
-
-    def inplane(e, edge):
-        ex = e + jnp.where(lane == 0, edge, pltpu.roll(e, 1, 1))
-        return ex + jnp.where(rowi == 0, 0.0, pltpu.roll(ex, 1, 0))
-
-    def flat(z):
-        T[z + 1] = inplane(E[z + 1], pltpu.roll(s["XE"][...], lax.rem(WID - z, WID), 1))
-
-    def start(z):
-        inv = 1.0 / (DIAG * (T[z] + T[z + 1]))
-        Q[z] = (1.0 - fixed[0, z].astype(F32)) * inv
-        for c in range(3):
-            s0[c, z + 1] = R[c, z] * inv
-
-    c_xe.wait_recv()
-    s["XE"][...] = unturned(s["XEr"], 8) * has_left
-    flat(DEP - 1)
-    flat(DEP - 2)
-    start(DEP - 1)
-    c_s = remote(s0.at[:, DEP], s0.at[:, 0], device(0, 1))
-    flat(0)
-    c_t = remote(T.at[1], T.at[DEP + 1], device(0, -1))
-    pl.loop(1, DEP - 2)(flat)
-    pl.loop(1, DEP - 1)(start)
-
-    def columns(planes, name):
-        slots = [((c, zz), 16 * c + zz) for c in range(3) for zz in planes]
-        first = pack(lambda i: s0[i[0], i[1]], slots, 0)
-        last = pack(lambda i: s0[i[0], i[1]], slots, WID - 1)
-        s["XLs" + name][...] = turned(first)[:48]
-        s["XRs" + name][...] = turned(last)[:48]
-        return first, (remote(s["XLs" + name], s["XRr" + name], device(-1)),
-                       remote(s["XRs" + name], s["XLr" + name], device(1)))
-
-    first, pair = columns(range(2, 9), "1")
-    s["X0"][...] = first
 
     far_y = jnp.abs(lax.broadcasted_iota(jnp.int32, (HEI, HEI), 0) - lax.broadcasted_iota(jnp.int32, (HEI, HEI), 1))
     s["Wy"][0], s["Wy"][1] = split(tap(far_y))
@@ -303,6 +223,89 @@
         s["Wx"][1 + j, 0], s["Wx"][1 + j, 1] = split(left)
         s["Wx"][5 + j, 0], s["Wx"][5 + j, 1] = split(right)
     s["W2"][...] = kept(gx * WID + lane, GX * WID) * kept(rowi, HEI)
+
+    s["WZ"][...] = kept(slab * DEP + lax.broadcasted_iota(jnp.int32, (DEP, WID), 0), S * DEP)
+
+    E, R = s["E"], s["R"]
+    loads[0].wait()
+    loads[1].wait()
+
+    @pl.loop(0, DEP)
+    def _(z):
+        b = bone[0, z].astype(F32)
+        d = dens[0, z]
+        E[z + 1] = b * d * d + (1.0 - b) * MARROW
+
+    def pack(get, slots, src):
+        acc = jnp.zeros((HEI, WID), F32)
+        for index, k in slots:
+            acc = jnp.where(lane == k, pltpu.roll(get(index), (k - src) % WID, 1), acc)
+        return acc
+
+    def turned(acc):
+        full = jnp.concatenate([acc, jnp.zeros((WID - HEI, WID), F32)], axis=0)
+        return jnp.transpose(full)
+
+    def unturned(ref, number):
+        got = ref[...]
+        full = jnp.concatenate([got, jnp.zeros((WID - number, WID), F32)], axis=0)
+        return jnp.transpose(full)[:HEI]
+
+    s["XEs"][...] = turned(pack(lambda z: E[z + 1], [(z, z) for z in range(DEP)], WID - 1))[:8]
+    loads[2].wait()
+    loads[3].wait()
+
+    @pl.loop(0, DEP)
+    def _(z):
+        f = 1.0 - fixed[0, z].astype(F32)
+        for c in range(3):
+            R[c, z] = f * load[c, 0, z]
+        s["GD"][z] = 0.5 * E[z + 1] / dens[0, z]
+
+    pl.semaphore_wait(barrier, len(peers))
+    c_xe = remote(s["XEs"], s["XEr"], device(1))
+    c_e = remote(E.at[DEP], E.at[0], device(0, 1))
+    c_r = remote(R.at[:, 0], s["R8"], device(0, -1))
+    c_xd = remote(s["XEs"], s["XDr"], device(1, 1))
+
+    T = s["T"]
+    s0, Q = s["s0"], s["Q"]
+
+    def inplane(e, edge):
+        ex = e + jnp.where(lane == 0, edge, pltpu.roll(e, 1, 1))
+        return ex + jnp.where(rowi == 0, 0.0, pltpu.roll(ex, 1, 0))
+
+    def flat(z):
+        T[z + 1] = inplane(E[z + 1], pltpu.roll(s["XE"][...], lax.rem(WID - z, WID), 1))
+
+    def start(z):
+        inv = 1.0 / (DIAG * (T[z] + T[z + 1]))
+        Q[z] = (1.0 - fixed[0, z].astype(F32)) * inv
+        for c in range(3):
+            s0[c, z + 1] = R[c, z] * inv
+
+    c_xe.wait_recv()
+    s["XE"][...] = unturned(s["XEr"], 8) * has_left
+    flat(DEP - 1)
+    flat(DEP - 2)
+    start(DEP - 1)
+    c_s = remote(s0.at[:, DEP], s0.at[:, 0], device(0, 1))
+    flat(0)
+    c_t = remote(T.at[1], T.at[DEP + 1], device(0, -1))
+    pl.loop(1, DEP - 2)(flat)
+    pl.loop(1, DEP - 1)(start)
+
+    def columns(planes, name):
+        slots = [((c, zz), 16 * c + zz) for c in range(3) for zz in planes]
+        first = pack(lambda i: s0[i[0], i[1]], slots, 0)
+        last = pack(lambda i: s0[i[0], i[1]], slots, WID - 1)
+        s["XLs" + name][...] = turned(first)[:48]
+        s["XRs" + name][...] = turned(last)[:48]
+        return first, (remote(s["XLs" + name], s["XRr" + name], device(-1)),
+                       remote(s["XRs" + name], s["XLr" + name], device(1)))
+
+    first, pair = columns(range(2, 9), "1")
+    s["X0"][...] = first
 
     def edges(got):
         for c in range(3):
@@ -437,7 +440,20 @@
         s0[c, DEP + 1] = s["R8"][c] * inv8
     c_s.wait_recv()
 
+    SDs, SDw, SE = s["SDs"], s["SDw"], s["SE"]
+
+    def self_energy(low, high):
+        def step(y0):
+            def plane(z, lo):
+                hi = planar(SDs, z + 2, y0)
+                m = zmodes(lo, hi)
+                SE[0, z, pl.ds(y0, 8)] = bilinear(m, stress(m))
+                return tuple(hi)
+            lax.fori_loop(low, high, plane, tuple(planar(SDs, low + 1, y0)))
+        return step
+
     first, pair = columns((0, 1, 9), "2")
+    chunks(self_energy(1, DEP - 1))
     s["X0"][...] = s["X0"][...] + first
     edges(s["XL1"][...] + arrive(pair, "2"))
     for zz in (0, 1, 9):
@@ -464,47 +480,29 @@
     c_xw = remote(s["XWs"], s["XWr"].at[pl.ds(0, 64)], device(-1))
     c_xc = remote(s["XWs"].at[pl.ds(0, 8)], s["XCr"], device(-1, -1))
 
-    SDs, SDw, SE = s["SDs"], s["SDw"], s["SE"]
-
-    def self_energy(y0):
-        def plane(z, lo):
-            hi = planar(SDs, z + 2, y0)
-            m = zmodes(lo, hi)
-            SE[0, z, pl.ds(y0, 8)] = bilinear(m, stress(m))
-            return tuple(hi)
-        lax.fori_loop(0, DEP, plane, tuple(planar(SDs, 1, y0)))
-
-    def w_energy(low, high):
-        def step(y0):
-            def plane(z, lo):
-                hi = planar(SDw, z + 1, y0)
-                m = zmodes(lo, hi)
-                SE[2, z, pl.ds(y0, 8)] = bilinear(m, stress(m))
-                return tuple(hi)
-            lax.fori_loop(low, high, plane, tuple(planar(SDw, low, y0)))
-        return step
-
-    def cross_energy(low, high):
+    def energies(low, high):
         def step(y0):
             def plane(z, carry):
                 los, lows = carry
                 his, hiw = planar(SDs, z + 2, y0), planar(SDw, z + 1, y0)
-                SE[1, z, pl.ds(y0, 8)] = bilinear(zmodes(lows, hiw), stress(zmodes(los, his)))
+                m = zmodes(lows, hiw)
+                f = stress(m)
+                SE[2, z, pl.ds(y0, 8)] = bilinear(m, f)
+                SE[1, z, pl.ds(y0, 8)] = bilinear(zmodes(los, his), f)
                 return tuple(his), tuple(hiw)
             lax.fori_loop(low, high, plane, (tuple(planar(SDs, low + 1, y0)), tuple(planar(SDw, low, y0))))
         return step
 
     def per_density(z, sums):
         zeta, m0, m1, m2 = sums
-        e = E[z + 1]
-        g = 0.5 * e / dens[0, z]
-        weight = s["W2"][...] * kept(jnp.full((HEI, WID), slab * DEP + z, jnp.int32), S * DEP)
-        zeta = zeta + fold(SE[2, z] * e)
+        g = s["GD"][z]
+        zeta = zeta + fold(SE[2, z] * E[z + 1])
+        share = s["WZ"][pl.ds(z, 1)]
         out = []
         for i, m in enumerate((m0, m1, m2)):
             v = SE[i, z] * g
             SE[i, z] = v
-            out.append(m + fold(v * weight))
+            out.append(m + share * fold(v * s["W2"][...]))
         return (zeta, *out)
 
     HLs, HRs, HLr, HRr = s["HLs"], s["HRs"], s["HLr"], s["HRr"]
@@ -524,12 +522,16 @@
             HRs[b, i] = acc_r
         return remote(HLs.at[b], HRr.at[b], device(-1)), remote(HRs.at[b], HLr.at[b], device(1))
 
-    chunks(self_energy)
+    @pl.loop(0, HEI // 8)
+    def _(i):
+        y0 = pl.multiple_of(i * 8, 8)
+        self_energy(0, 1)(y0)
+        self_energy(DEP - 1, DEP)(y0)
+
     c_xw.wait_recv()
     s["XH"][...] = unturned(s["XWr"], 72) * has_right
     pl.loop(0, DEP)(lambda z: xstage(w0, SDw, place_w, z))
-    chunks(w_energy(0, DEP - 1))
-    chunks(cross_energy(0, DEP - 1))
+    chunks(energies(0, DEP - 1))
     forms = lax.fori_loop(0, DEP - 1, per_density, (zero8,) * 4)
     sides = [send_sides(0)]
 
@@ -540,8 +542,7 @@
     for c in range(3):
         w0[c, DEP] = w0[c, DEP] * has_up
     xstage(w0, SDw, place_w, DEP)
-    chunks(w_energy(DEP - 1, DEP))
-    chunks(cross_energy(DEP - 1, DEP))
+    chunks(energies(DEP - 1, DEP))
     forms = per_density(DEP - 1, forms)
 
     axes = ((GX, gx, lambda p: (p, gy, gz)), (GY, gy, lambda p: (gx, p, gz)), (GZ, gz, lambda p: (gx, gy, p)))
@@ -630,14 +631,14 @@
     RU, RD = s["RU"], s["RD"]
     RU[0] = low
     RD[0] = high
-    c_u0 = remote(RU.at[0], RU.at[1], device(0, -1))
-    c_d0 = remote(RD.at[0], RD.at[1], device(0, 1))
+    near = [remote(RU.at[0], RU.at[1], device(0, -1)), remote(RD.at[0], RD.at[1], device(0, 1)),
+            remote(RU.at[0], RU.at[2], device(0, -2)), remote(RD.at[0], RD.at[2], device(0, 2))]
 
     def planes(k):
         z = DEP - 1 - k
         return remote(G.at[k], Gup.at[k], device(0, -3)), remote(G.at[z], Gdn.at[z], device(0, 3))
 
-    far = [planes(k) for k in range(4)]
+    far = [planes(k) for k in range(DEP)]
 
     acc = None
     for z in range(DEP):
@@ -648,15 +649,8 @@
         acc = LAMBDA * (acc + G[z + 1])
         F[z] = F[z] + acc
 
-    at1, at3 = flag(slab + 1 < S), flag(slab + 3 < S)
-    bt1, bt3 = flag(slab >= 1), flag(slab >= 3)
-    c_u0.wait_recv()
-    c_d0.wait_recv()
-    RU[2] = RU[0] + (LAMBDA**DEP * at1) * RU[1]
-    RD[2] = RD[0] + (LAMBDA**DEP * bt1) * RD[1]
-    c_u1 = remote(RU.at[2], RU.at[3], device(0, -1))
-    c_d1 = remote(RD.at[2], RD.at[3], device(0, 1))
-    far += [planes(k) for k in range(4, DEP)]
+    at1, at2, at3 = flag(slab + 1 < S), flag(slab + 2 < S), flag(slab + 3 < S)
+    bt1, bt2, bt3 = flag(slab >= 1), flag(slab >= 2), flag(slab >= 3)
 
     @pl.loop(0, DEP)
     def _(z):
@@ -666,9 +660,10 @@
     stores = [pltpu.make_async_copy(s["U"], out_u, s["local"].at[4])]
     stores[0].start()
 
-    c_u1.wait_recv()
-    c_d1.wait_recv()
-    near_u, near_d = at1 * RU[3], bt1 * RD[3]
+    for copy in near:
+        copy.wait_recv()
+    near_u = at1 * RU[1] + (LAMBDA**DEP * at2) * RU[2]
+    near_d = bt1 * RD[1] + (LAMBDA**DEP * bt2) * RD[2]
     for z in range(DEP):
         F[z] = F[z] + LAMBDA ** (DEP - z) * near_u + LAMBDA ** (z + 1) * near_d
 
@@ -731,11 +726,11 @@
         "XLs2": V(thin, F32), "XRs2": V(thin, F32), "XLr2": V(thin, F32), "XRr2": V(thin, F32),
         "XWs": V((64, WID), F32), "XWr": V((72, WID), F32), "XCr": V((8, WID), F32),
         "SE": V((3, DEP, *plane), F32), "own": V((3, 8, WID), F32), "red": V((3, max(sizes), 8, WID), F32),
-        "Wy": V((2, HEI, HEI), BF16), "Wx": V((9, 2, WID, WID), BF16), "W2": V(plane, F32),
+        "Wy": V((2, HEI, HEI), BF16), "Wx": V((9, 2, WID, WID), BF16), "W2": V(plane, F32), "WZ": V((DEP, WID), F32), "GD": V((DEP, *plane), F32),
         "G": V((DEP, *plane), F32), "Gup": V((DEP, *plane), F32), "Gdn": V((DEP, *plane), F32),
         "HLs": V((2, 3, *plane), F32), "HRs": V((2, 3, *plane), F32),
         "HLr": V((2, 3, *plane), F32), "HRr": V((2, 3, *plane), F32),
-        "RU": V((4, *plane), F32), "RD": V((4, *plane), F32), "F": V((DEP, *plane), F32), "RR": V((2, *plane), F32),
+        "RU": V((3, *plane), F32), "RD": V((3, *plane), F32), "F": V((DEP, *plane), F32), "RR": V((2, *plane), F32),
     }
     names = list(scratch)
 

time: 95.8 us -> 90.6 us (0.946)
  the two profiles are of different devices: /device:TPU:6 before, /device:TPU:1 now
where the time goes in v3:
time: 90.6 us; the launch traced here: 90.4 us
  Pallas kernels  85.7 us (95%)
  local copies, waits for them, and re-layouts  4.13 us (5%)
    pallas_call x1, Pallas kernels, on_device(): pl.pallas_call(kernel, out_shape=(jax.ShapeDtypeStruct(density.shape, F32...  85.7 us
    unnamed x2, local copies, waits for them, and re-layouts  4.13 us

profile of v3, /device:TPU:1, one launch (start us, length us, event | category | flops | bytes accessed | tf_op | source)
XLA Modules:
  0.0 90.4 jit_solution(2418647654397182249)
XLA Ops:
  0.6 85.7 %shard_map.59 = (f32[1,8,96,128]{3,2,1,0:T(8,128)}, f32[3,1,8,96,128]{4,3,2,1,0:T(8,128)}) custom-call(f32[1,8,96,128]{3,2,1,0:T(8,128)} %refs_0_.1, s32[1,8,96,128]{3,2,1,0:T(8,128)} %refs_1_.1, s32[1,8,96,128]{3,2,1,0:T(8,128)} %refs_2_.1, f32[3,1,8,96,128]{4,3,2,1,0:T(8,128)} %refs_3_.1), custom_call_target="tpu_custom_call" | custom-call | tf_op jit(solution)/shard_map/pallas_call | solution.py:741
  86.3 1.8 %copy.8 = f32[1,8,96,128]{3,2,1,0:T(8,128)} copy(f32[1,8,96,128]{3,2,1,0:T(8,128)} %get-tuple-element.4) | data formatting | bytes 786432
  88.1 2.4 %copy.9 = f32[3,1,8,96,128]{4,3,2,1,0:T(8,128)} copy(f32[3,1,8,96,128]{4,3,2,1,0:T(8,128)} %get-tuple-element.5) | data formatting | bytes 2359296

commit v4 on v3

--- a/solution.py
+++ b/solution.py
@@ -188,12 +188,15 @@
     barrier = pltpu.get_barrier_semaphore()
     peers = [device(-1), device(1), device(0, 1), device(0, -1), device(1, 1), device(-1, -1),
              device(0, 3), device(0, -3), device(0, 2), device(0, -2)]
-    for k in range(2, GX - 1):
-        peers.append((lax.rem(gx + k, GX), gy, gz))
-    for k in range(1, GY):
-        peers.append((gx, lax.rem(gy + k, GY), gz))
-    for k in range(1, GZ):
-        peers.append((gx, gy, lax.rem(gz + k, GZ)))
+    NY = GZ // 2
+    lo, iy = lax.div(gz, NY), lax.rem(gz, NY)
+    axes = ((GX, gx, lambda p: (p, gy, gz)),
+            (2 * GY, 2 * gy + lo, lambda p: (gx, lax.div(p, 2), lax.rem(p, 2) * NY + iy)),
+            (NY, iy, lambda p: (gx, gy, lo * NY + p)))
+    for number, me, target in axes:
+        for k in range(1, number):
+            if me is not gx or 1 < k < GX - 1:
+                peers.append(target(lax.rem(me + k, number)))
     for peer in peers:
         pl.semaphore_signal(barrier, inc=1, device_id=peer, device_id_type=MESH)
 
@@ -545,25 +548,29 @@
     chunks(energies(DEP - 1, DEP))
     forms = per_density(DEP - 1, forms)
 
-    axes = ((GX, gx, lambda p: (p, gy, gz)), (GY, gy, lambda p: (gx, p, gz)), (GZ, gz, lambda p: (gx, gy, p)))
     own, red = s["own"], s["red"]
 
-    def reduce_start(stage):
+    def reduce_start(stage, row):
+        own[stage, pl.ds(0, 1)] = row
         n, me, target = axes[stage]
-        return [remote(own.at[stage], red.at[stage, me], target(lax.rem(me + k, n))) for k in range(1, n)]
+        return [remote(own.at[stage, pl.ds(0, 1)], red.at[stage, me, pl.ds(0, 1)], target(lax.rem(me + k, n)))
+                for k in range(1, n)]
 
     def reduce_end(stage, copies):
         n, me, _ = axes[stage]
         for copy in copies:
             copy.wait_recv()
-        red[stage, me] = own[stage]
-        total = red[stage, 0]
+        red[stage, me, pl.ds(0, 1)] = own[stage, pl.ds(0, 1)]
+        total = red[stage, 0, pl.ds(0, 1)]
         for k in range(1, n):
-            total = total + red[stage, k]
+            total = total + red[stage, k, pl.ds(0, 1)]
         return total
 
-    own[0] = jnp.concatenate([rows(v) for v in (gamma, delta, eps, *forms)] + [jnp.zeros((1, WID), F32)], axis=0)
-    copies = reduce_start(0)
+    lane1 = lax.broadcasted_iota(jnp.int32, (1, WID), 1)
+    mine = jnp.zeros((1, WID), F32)
+    for k, v in enumerate((gamma, delta, eps, *forms)):
+        mine = jnp.where(lane1 == k, jnp.sum(rows(v), axis=1, keepdims=True), mine)
+    copies = reduce_start(0, mine)
     sides.append(send_sides(1))
 
     def smooth_y(v):
@@ -579,8 +586,7 @@
         for i in range(3):
             SE[i, z] = smooth_y(SE[i, z])
 
-    own[1] = reduce_end(0, copies)
-    copies = reduce_start(1)
+    copies = reduce_start(1, reduce_end(0, copies))
 
     for pair in sides:
         for copy in pair:
@@ -591,8 +597,7 @@
             HLr[b, i] = smooth_y(HLr[b, i] * has_left)
             HRr[b, i] = smooth_y(HRr[b, i] * has_right)
 
-    own[2] = reduce_end(1, copies)
-    copies = reduce_start(2)
+    copies = reduce_start(2, reduce_end(1, copies))
 
     for b in range(2):
         @pl.loop(0, 4)
@@ -601,8 +606,8 @@
                 SE[i, 4 * b + j] = (smooth_x(SE[i, 4 * b + j], 0) + smooth_x(HLr[b, i], 1 + j)
                                     + smooth_x(HRr[b, i], 5 + j))
 
-    total = jnp.sum(reduce_end(2, copies), axis=1, keepdims=True)
-    g0, d0, ep, ze = total[0:1], total[1:2], total[2:3], total[3:4]
+    total = reduce_end(2, copies)
+    g0, d0, ep, ze, t0, t1, t2 = (total[:, k:k + 1] for k in range(7))
     alpha = g0 / d0
     g1 = g0 - 2.0 * alpha * d0 + alpha * alpha * ep
     beta = g1 / g0
@@ -613,15 +618,24 @@
     ca = jnp.broadcast_to(a1, (HEI, WID))
     cb = jnp.broadcast_to(b1, (HEI, WID))
     caa, cab, cbb = a1 * a1, 2.0 * (a1 * b1), b1 * b1
-    mean = (caa * total[4:5] + cab * total[5:6] + cbb * total[6:7]) / float(S * DEP * HEI * WID * GX)
+    mean = (caa * t0 + cab * t1 + cbb * t2) / float(S * DEP * HEI * WID * GX)
     scale = NORMAL * jnp.broadcast_to(1.0 / (mean + EPSILON), (HEI, WID))
     caa, cab, cbb = (jnp.broadcast_to(v, (HEI, WID)) for v in (caa, cab, cbb))
 
     G, Gup, Gdn, F = s["G"], s["Gup"], s["Gdn"], s["F"]
 
-    @pl.loop(0, DEP)
-    def _(z):
+    def planes(k):
+        z = DEP - 1 - k
+        return remote(G.at[k], Gup.at[k], device(0, -3)), remote(G.at[z], Gdn.at[z], device(0, 3))
+
+    def combine(z):
         G[z] = caa * SE[0, z] + cab * SE[1, z] + cbb * SE[2, z]
+
+    far = []
+    for k in range(DEP // 2):
+        combine(k)
+        combine(DEP - 1 - k)
+        far.append(planes(k))
 
     low = G[DEP - 1]
     high = G[0]
@@ -633,12 +647,7 @@
     RD[0] = high
     near = [remote(RU.at[0], RU.at[1], device(0, -1)), remote(RD.at[0], RD.at[1], device(0, 1)),
             remote(RU.at[0], RU.at[2], device(0, -2)), remote(RD.at[0], RD.at[2], device(0, 2))]
-
-    def planes(k):
-        z = DEP - 1 - k
-        return remote(G.at[k], Gup.at[k], device(0, -3)), remote(G.at[z], Gdn.at[z], device(0, 3))
-
-    far = [planes(k) for k in range(DEP)]
+    far += [planes(k) for k in range(DEP // 2, DEP)]
 
     acc = None
     for z in range(DEP):
@@ -704,7 +713,7 @@
 
 def on_device(sizes, density, bone, fixed, load):
     GX, GY, GZ = sizes
-    copies = 4 + 2 + 4 + 3 + 4 + (GX + GY + GZ - 3) + 4 + 16
+    copies = 4 + 2 + 4 + 3 + 4 + (GX + 2 * GY + GZ // 2 - 3) + 4 + 16
     V = pltpu.VMEM
     plane, tall, thin = (HEI, WID), (HEI + 8, WID), (48, WID)
     scratch = {
@@ -725,7 +734,7 @@
         "XLs1": V(thin, F32), "XRs1": V(thin, F32), "XLr1": V(thin, F32), "XRr1": V(thin, F32),
         "XLs2": V(thin, F32), "XRs2": V(thin, F32), "XLr2": V(thin, F32), "XRr2": V(thin, F32),
         "XWs": V((64, WID), F32), "XWr": V((72, WID), F32), "XCr": V((8, WID), F32),
-        "SE": V((3, DEP, *plane), F32), "own": V((3, 8, WID), F32), "red": V((3, max(sizes), 8, WID), F32),
+        "SE": V((3, DEP, *plane), F32), "own": V((3, 8, WID), F32), "red": V((3, max(GX, 2 * GY, GZ // 2), 8, WID), F32),
         "Wy": V((2, HEI, HEI), BF16), "Wx": V((9, 2, WID, WID), BF16), "W2": V(plane, F32), "WZ": V((DEP, WID), F32), "GD": V((DEP, *plane), F32),
         "G": V((DEP, *plane), F32), "Gup": V((DEP, *plane), F32), "Gdn": V((DEP, *plane), F32),
         "HLs": V((2, 3, *plane), F32), "HRs": V((2, 3, *plane), F32),
@@ -738,7 +747,7 @@
         body(sizes, *refs[:6], dict(zip(names, refs[6:])))
 
     outer = pl.BlockSpec(memory_space=pltpu.HBM)
-    return pl.pallas_call(
+    results = pl.pallas_call(
         kernel,
         out_shape=(jax.ShapeDtypeStruct(density.shape, F32), jax.ShapeDtypeStruct(load.shape, F32)),
         in_specs=[outer] * 4,
@@ -747,6 +756,23 @@
         compiler_params=pltpu.CompilerParams(
             collective_id=0, has_side_effects=True, vmem_limit_bytes=56 * 1024 * 1024),
     )(density, bone, fixed, load)
+
+    def hand_over(d, u, out_d, out_u, sem):
+        moves = [pltpu.make_async_copy(d.at[0, pl.ds(4 * k, 4)], out_d.at[0, pl.ds(4 * k, 4)], sem.at[k]) for k in range(2)]
+        moves += [pltpu.make_async_copy(u.at[c, 0, pl.ds(4 * k, 4)], out_u.at[c, 0, pl.ds(4 * k, 4)], sem.at[2 + 2 * c + k])
+                  for c in range(3) for k in range(2)]
+        for move in moves:
+            move.start()
+        for move in moves:
+            move.wait()
+
+    return pl.pallas_call(
+        hand_over,
+        out_shape=tuple(jax.ShapeDtypeStruct(v.shape, F32) for v in results),
+        in_specs=[outer] * 2,
+        out_specs=(outer, outer),
+        scratch_shapes=[pltpu.SemaphoreType.DMA((8,))],
+    )(*results)
 
 
 def solution(mesh):

time: 90.6 us -> 135 us (1.49); the launches traced: 90.4 us -> 133 us
  Pallas kernels: 85.7 us -> 132 us
  local copies, waits for them, and re-layouts: 4.13 us -> 0 us
    pallas_call x0 -> x1, Pallas kernels: none -> 48.8 us  [on_device(): pl.pallas_call(hand_over, out_shape=tuple((jax.ShapeDtypeStruct(v.shape,...]
    unnamed x2 -> x0, local copies, waits for them, and re-layouts: 4.13 us -> none
    pallas_call x1, Pallas kernels: 85.7 us -> 83.3 us  [on_device(): pl.pallas_call(kernel, out_shape=(jax.ShapeDtypeStruct(density.shape, F32...]
where the time goes in v4:
time: 135 us; the launch traced here: 133 us
  Pallas kernels  132 us (98%)
    pallas_call x1, Pallas kernels, on_device(): pl.pallas_call(kernel, out_shape=(jax.ShapeDtypeStruct(density.shape, F32...  83.3 us
    pallas_call x1, Pallas kernels, on_device(): pl.pallas_call(hand_over, out_shape=tuple((jax.ShapeDtypeStruct(v.shape,...  48.8 us

profile of v4, /device:TPU:1, one launch (start us, length us, event | category | flops | bytes accessed | tf_op | source)
XLA Modules:
  0.0 132.7 jit_solution(6206295787388497365)
XLA Ops:
  0.6 83.3 %shard_map.59 = (f32[1,8,96,128]{3,2,1,0:T(8,128)}, f32[3,1,8,96,128]{4,3,2,1,0:T(8,128)}) custom-call(f32[1,8,96,128]{3,2,1,0:T(8,128)} %refs_0_.1, s32[1,8,96,128]{3,2,1,0:T(8,128)} %refs_1_.1, s32[1,8,96,128]{3,2,1,0:T(8,128)} %refs_2_.1, f32[3,1,8,96,128]{4,3,2,1,0:T(8,128)} %refs_3_.1), custom_call_target="tpu_custom_call" | custom-call | tf_op jit(solution)/shard_map/pallas_call | solution.py:750
  83.9 48.8 %shard_map.60 = (f32[1,8,96,128]{3,2,1,0:T(8,128)}, f32[3,1,8,96,128]{4,3,2,1,0:T(8,128)}) custom-call(f32[1,8,96,128]{3,2,1,0:T(8,128)} %get-tuple-element.4.d, f32[3,1,8,96,128]{4,3,2,1,0:T(8,128)} %get-tuple-element.5.u), custom_call_target="tpu_custom_call" | custom-call | tf_op jit(solution)/shard_map/pallas_call | solution.py:769

commit v5 on v4

--- a/solution.py
+++ b/solution.py
@@ -19,6 +19,7 @@
 DEP = 8
 HEI = 96
 WID = 128
+PIECES = 1
 F32 = jnp.float32
 BF16 = jnp.bfloat16
 
@@ -757,21 +758,30 @@
             collective_id=0, has_side_effects=True, vmem_limit_bytes=56 * 1024 * 1024),
     )(density, bone, fixed, load)
 
-    def hand_over(d, u, out_d, out_u, sem):
-        moves = [pltpu.make_async_copy(d.at[0, pl.ds(4 * k, 4)], out_d.at[0, pl.ds(4 * k, 4)], sem.at[k]) for k in range(2)]
-        moves += [pltpu.make_async_copy(u.at[c, 0, pl.ds(4 * k, 4)], out_u.at[c, 0, pl.ds(4 * k, 4)], sem.at[2 + 2 * c + k])
-                  for c in range(3) for k in range(2)]
-        for move in moves:
-            move.start()
-        for move in moves:
-            move.wait()
+    def hand_over(d, u, out_d, out_u, mid_d, mid_u, into, out):
+        parts = []
+        for k in range(PIECES):
+            rows_z = pl.ds(k * (DEP // PIECES), DEP // PIECES)
+            parts.append((d.at[0, rows_z], mid_d.at[0, rows_z], out_d.at[0, rows_z]))
+            parts += [(u.at[c, 0, rows_z], mid_u.at[c, 0, rows_z], out_u.at[c, 0, rows_z]) for c in range(3)]
+        reads = [pltpu.make_async_copy(a, b, into.at[n]) for n, (a, b, _) in enumerate(parts)]
+        writes = [pltpu.make_async_copy(b, c, out.at[n]) for n, (_, b, c) in enumerate(parts)]
+        for read in reads:
+            read.start()
+        for read, write in zip(reads, writes):
+            read.wait()
+            write.start()
+        for write in writes:
+            write.wait()
 
     return pl.pallas_call(
         hand_over,
         out_shape=tuple(jax.ShapeDtypeStruct(v.shape, F32) for v in results),
         in_specs=[outer] * 2,
         out_specs=(outer, outer),
-        scratch_shapes=[pltpu.SemaphoreType.DMA((8,))],
+        scratch_shapes=[V(density.shape, F32), V(load.shape, F32), pltpu.SemaphoreType.DMA((4 * PIECES,)),
+                        pltpu.SemaphoreType.DMA((4 * PIECES,))],
+        compiler_params=pltpu.CompilerParams(vmem_limit_bytes=56 * 1024 * 1024),
     )(*results)
 
 

time: 135 us -> 88.2 us (0.65)
  the two profiles are of different devices: /device:TPU:1 before, /device:TPU:120 now
where the time goes in v5:
time: 88.2 us; the launch traced here: 88.1 us
  Pallas kernels  87.4 us (99%)
    pallas_call x1, Pallas kernels, on_device(): pl.pallas_call(kernel, out_shape=(jax.ShapeDtypeStruct(density.shape, F32...  85.2 us
    pallas_call x1, Pallas kernels, on_device(): pl.pallas_call(hand_over, out_shape=tuple((jax.ShapeDtypeStruct(v.shape,...  2.2 us

profile of v5, /device:TPU:120, one launch (start us, length us, event | category | flops | bytes accessed | tf_op | source)
XLA Modules:
  0.0 88.1 jit_solution(3746955659250023727)
XLA Ops:
  0.6 85.2 %shard_map.59 = (f32[1,8,96,128]{3,2,1,0:T(8,128)}, f32[3,1,8,96,128]{4,3,2,1,0:T(8,128)}) custom-call(f32[1,8,96,128]{3,2,1,0:T(8,128)} %refs_0_.1, s32[1,8,96,128]{3,2,1,0:T(8,128)} %refs_1_.1, s32[1,8,96,128]{3,2,1,0:T(8,128)} %refs_2_.1, f32[3,1,8,96,128]{4,3,2,1,0:T(8,128)} %refs_3_.1), custom_call_target="tpu_custom_call" | custom-call | tf_op jit(solution)/shard_map/pallas_call | solution.py:751
  85.9 2.2 %shard_map.60 = (f32[1,8,96,128]{3,2,1,0:T(8,128)}, f32[3,1,8,96,128]{4,3,2,1,0:T(8,128)}) custom-call(f32[1,8,96,128]{3,2,1,0:T(8,128)} %get-tuple-element.4.d, f32[3,1,8,96,128]{4,3,2,1,0:T(8,128)} %get-tuple-element.5.u), custom_call_target="tpu_custom_call" | custom-call | tf_op jit(solution)/shard_map/pallas_call | solution.py:777

commit v6 on v5

--- a/solution.py
+++ b/solution.py
@@ -460,7 +460,7 @@
     chunks(self_energy(1, DEP - 1))
     s["X0"][...] = s["X0"][...] + first
     edges(s["XL1"][...] + arrive(pair, "2"))
-    for zz in (0, 1, 9):
+    for zz in (0, 1):
         xstage(s0, s["SDs"], place_s, zz)
 
     def late(y0):
@@ -470,12 +470,18 @@
         down, above = element(n1, n2, 1, y0)
         put(both(up, down), 1, y0)
         put(above, 2, y0, more=True)
-        put(element(planar(SD, 8, y0), planar(SD, 9, y0), DEP, y0)[0], DEP, y0, more=True)
         edge_elements(y0)
 
     chunks(late)
     sums = image(0, sums)
     c_w = remote(w0.at[:, 0], w0.at[:, DEP], device(0, -1))
+    xstage(s0, s["SDs"], place_s, DEP + 1)
+
+    def last_element(y0):
+        SD = s["SDs"]
+        put(element(planar(SD, DEP, y0), planar(SD, DEP + 1, y0), DEP, y0)[0], DEP, y0, more=True)
+
+    chunks(last_element)
     sums = image(1, sums)
     gamma, delta, eps = image(DEP - 1, sums)
 

time: 88.2 us -> 88.4 us (level)
  no operation moved by 1% of the time
where the time goes in v6:
time: 88.4 us; the launch traced here: 88.2 us
  Pallas kernels  87.6 us (99%)
    pallas_call x1, Pallas kernels, on_device(): pl.pallas_call(kernel, out_shape=(jax.ShapeDtypeStruct(density.shape, F32...  85.4 us
    pallas_call x1, Pallas kernels, on_device(): pl.pallas_call(hand_over, out_shape=tuple((jax.ShapeDtypeStruct(v.shape,...  2.2 us

profile of v6, /device:TPU:120, one launch (start us, length us, event | category | flops | bytes accessed | tf_op | source)
XLA Modules:
  0.0 88.2 jit_solution(15411747734534385849)
XLA Ops:
  0.6 85.4 %shard_map.59 = (f32[1,8,96,128]{3,2,1,0:T(8,128)}, f32[3,1,8,96,128]{4,3,2,1,0:T(8,128)}) custom-call(f32[1,8,96,128]{3,2,1,0:T(8,128)} %refs_0_.1, s32[1,8,96,128]{3,2,1,0:T(8,128)} %refs_1_.1, s32[1,8,96,128]{3,2,1,0:T(8,128)} %refs_2_.1, f32[3,1,8,96,128]{4,3,2,1,0:T(8,128)} %refs_3_.1), custom_call_target="tpu_custom_call" | custom-call | tf_op jit(solution)/shard_map/pallas_call | solution.py:757
  86.0 2.2 %shard_map.60 = (f32[1,8,96,128]{3,2,1,0:T(8,128)}, f32[3,1,8,96,128]{4,3,2,1,0:T(8,128)}) custom-call(f32[1,8,96,128]{3,2,1,0:T(8,128)} %get-tuple-element.4.d, f32[3,1,8,96,128]{4,3,2,1,0:T(8,128)} %get-tuple-element.5.u), custom_call_target="tpu_custom_call" | custom-call | tf_op jit(solution)/shard_map/pallas_call | solution.py:783
